TPU v7x, 128 devices: a whole 4x4x4 slice. The times are simulated.
128 devices in a mesh: gx: 8 (over z, core), gy: 16 (over x, y).
Axes of the slice: x: 4, y: 4, z: 4, core: 2. Of those that a mesh axis runs over, the one named last changes fastest.
Arguments:
- grad_out: bfloat16 [1048576, 128], P(('gx', 'gy')), may hold values from -6 to 6
- preact: bfloat16 [1048576, 128], P(('gx', 'gy')), may hold values from -6 to 6
- features: bfloat16 [1048576, 128], P(('gx', 'gy')), may hold values from -6 to 6
- neighbour_mean: bfloat16 [1048576, 128], P(('gx', 'gy')), may hold values from -6 to 6
- w_self: bfloat16 [128, 128], replicated, may hold values from -0.5 to 0.5
- w_neigh: bfloat16 [128, 128], replicated, may hold values from -0.5 to 0.5
- degrees: int32 [1048576], P(('gx', 'gy')), may hold values from 8 to 63
- tile_values: bfloat16 [49152, 128, 128], P(('gx', 'gy')), may hold values from 0.0099487305 to 1
- tile_list: int32 [128, 2, 384], P(('gx', 'gy')), may hold values from 0 to 8191, as said below
- send_counts: int32 [128, 128], P(('gx', 'gy')), may hold values from 0 to 3, as said below
Outputs:
- grad_features: bfloat16 [1048576, 128], P(('gx', 'gy'))
- grad_neighbour: bfloat16 [1048576, 128], P(('gx', 'gy'))
- grad_w_self: float32 [128, 128], replicated
- grad_w_neigh: float32 [128, 128], replicated
Inputs may be any that keep to these rules, and one draw needn't show every extreme that they name: `tile_list`: entry [i, 0, s] is a block row of device i's own range (i * 64 to i * 64 + 63); entry [i, 1, s] is a block column of the range of device s // 3. `send_counts`: every device uses all 3 slots for its own range; in every draw one device receives 3 used slots from every device.
All inputs are finite; a program needn't handle non-finite values.
Results may differ from a plain program's by a relative error of at most 0.0028.
Values may be sent and summed in bfloat16 or wider, within the bound.
No kernel may reach another device: no remote copies, remote signals or barrier semaphores. Data moves between devices by JAX's collectives and lax.ppermute only.
A program may use at most 192 MiB of HBM per device.

v0:
```python
import math

import jax
import jax.numpy as jnp
from jax import lax
from jax.sharding import PartitionSpec as P


def body(
    grad_out,
    preact,
    features,
    neighbour_mean,
    w_self,
    w_neigh,
    degrees,
    tile_values,
    tile_list,
    send_counts,
):
    feat_width = grad_out.shape[1]
    block_size = tile_values.shape[1]
    blocks_dev = grad_out.shape[0] // block_size
    size_major = lax.axis_size("gx")
    size_minor = lax.axis_size("gy")
    peer_count = size_major * size_minor
    capacity = tile_values.shape[0] // peer_count
    relu_grad = jnp.where(preact > 0, grad_out, jnp.zeros_like(grad_out))
    contract_out = (((1,), (1,)), ((), ()))
    neigh_grad = lax.dot_general(
        relu_grad, w_neigh, contract_out, preferred_element_type=jnp.float32
    )
    grad_neighbour = neigh_grad.astype(jnp.bfloat16)
    scaled_grad = (neigh_grad / degrees.astype(jnp.float32)[:, None]).astype(jnp.bfloat16)
    picked_rows = scaled_grad.reshape(blocks_dev, block_size, feat_width)[
        tile_list[0, 0] % blocks_dev
    ]
    slot_terms = jnp.einsum(
        "sij,sik->sjk", tile_values, picked_rows, preferred_element_type=jnp.float32
    )
    slot_ids = jnp.arange(peer_count * capacity, dtype=jnp.int32)
    slot_valid = slot_ids % capacity < send_counts[0][slot_ids // capacity]
    outgoing = jnp.where(slot_valid[:, None, None], slot_terms, jnp.zeros_like(slot_terms)).astype(
        jnp.bfloat16
    )
    columns = (tile_list[0, 1] % blocks_dev).astype(jnp.bfloat16)
    got_blocks, got_columns = (
        lax.all_to_all(
            outgoing.reshape(peer_count, capacity, block_size, feat_width),
            ("gx", "gy"),
            split_axis=0,
            concat_axis=0,
            tiled=True,
        ),
        lax.all_to_all(
            columns.reshape(peer_count, capacity),
            ("gx", "gy"),
            split_axis=0,
            concat_axis=0,
            tiled=True,
        ),
    )
    got_blocks = got_blocks.reshape(peer_count * capacity, block_size, feat_width)
    got_columns = got_columns.reshape(peer_count * capacity).astype(jnp.float32)
    block_ids = jnp.arange(blocks_dev, dtype=jnp.float32)
    one_hot = (got_columns[None, :] == block_ids[:, None]).astype(jnp.bfloat16)
    incoming = jnp.einsum("bs,sjk->bjk", one_hot, got_blocks, preferred_element_type=jnp.float32)
    self_grad = lax.dot_general(relu_grad, w_self, contract_out, preferred_element_type=jnp.float32)
    grad_features = (self_grad + incoming.reshape(blocks_dev * block_size, feat_width)).astype(
        jnp.bfloat16
    )
    grad_scale = 1.0 / math.sqrt(grad_out.shape[0] * peer_count)
    contract_rows = (((0,), (0,)), ((), ()))
    local_self = (
        lax.dot_general(features, relu_grad, contract_rows, preferred_element_type=jnp.float32)
        * grad_scale
    )
    local_neigh = (
        lax.dot_general(
            neighbour_mean, relu_grad, contract_rows, preferred_element_type=jnp.float32
        )
        * grad_scale
    )
    grad_w_self, grad_w_neigh = lax.psum((local_self, local_neigh), ("gx", "gy"))
    return (grad_features, grad_neighbour, grad_w_self, grad_w_neigh)


def solution(mesh):
    placed = (
        P(("gx", "gy"), None),
        P(("gx", "gy"), None),
        P(("gx", "gy"), None),
        P(("gx", "gy"), None),
        P(),
        P(),
        P(("gx", "gy")),
        P(("gx", "gy"), None, None),
        P(("gx", "gy"), None, None),
        P(("gx", "gy"), None),
    )
    return jax.shard_map(
        body,
        mesh=mesh,
        in_specs=placed,
        out_specs=(P(("gx", "gy"), None), P(("gx", "gy"), None), P(), P()),
        check_vma=False,
    )
```

profile of v0, /device:TPU:7, one launch (start us, length us, event | category | flops | bytes accessed | tf_op | source)
XLA Modules:
  0.0 369.5 jit_solution(16196833762482416085)
XLA Ops:
  7.2 0.0 copy-start
  7.2 0.9 slice_reduce_fusion
  8.0 0.2 squeeze.9
  8.2 0.1 copy.31
  8.3 0.8 copy.34
  9.1 10.8 %all-to-all-start = ((bf16[128,1,3]{2,1,0:T(2,128)(2,1)}), bf16[128,1,3]{2,1,0:T(2,128)(2,1)S(1)}, u32[]{:S(2)}, u32[]{:S(2)}) async-start(bf16[128,1,3]{2,1,0:T(2,128)(2,1)} %copy.34), calls=%async_computation | async-start | bytes 131072 | tf_op jit(solution)/shard_map/all_to_all | solution.py:55
  19.9 0.7 fusion.15
  20.7 0.8 convert_element_type.43
  21.4 3.4 gather_fusion
  24.9 0.0 copy-start.6
  24.9 2.5 compare_select_fusion
  27.4 0.0 copy-done.6
  27.4 0.0 copy-start.1
  27.4 4.8 %fusion.17 = (bf16[8192,128]{1,0:T(8,128)(2,1)}, bf16[8192,128]{1,0:T(8,128)(2,1)}) fusion(f32[8192]{0:T(1024)S(1)} %convert_element_type.43, bf16[8192,128]{1,0:T(8,128)(2,1)S(1)} %compare_select_fusion, bf16[128,128]{1,0:T(8,128)(2,1)S(1)} %copy-done.6), kind=kOutput, calls=%fused_computation.43 | convolution fusion | flops 271581184 | bytes 6356992 | tf_op jit(solution)/shard_map/dot_general | solution.py:30
  32.1 0.0 copy-done.1
  32.1 12.9 %gather_fusion.1 = bf16[384,128,128]{2,1,0:T(8,128)(2,1)} fusion(bf16[64,128,128]{2,1,0:T(8,128)(2,1)} %bitcast.27, s32[1024]{0:T(1024)S(1)} %pad_clamp_fusion), kind=kCustom, calls=%fused_computation.1 | custom fusion | bytes 25167360 | tf_op jit(solution)/shard_map/gather | solution.py:35
  45.1 16.5 %select_convert_fusion = bf16[384,128,128]{2,1,0:T(8,128)(2,1)} fusion(pred[384]{0:T(512)(128)(4,1)S(1)} %fusion.10, bf16[384,128,128]{2,1,0:T(8,128)(2,1)} %gather_fusion.1, bf16[384,128,128]{2,1,0:T(8,128)(2,1)} %param.17), kind=kOutput, calls=%fused_computation.2 | convolution fusion | flops 1623195648 | bytes 37749120 | tf_op jit(solution)/shard_map/sij,sik->sjk/dot_general | solution.py:38
  61.6 16.6 %copy.36 = bf16[128,3,128,128]{3,2,1,0:T(8,128)(2,1)} copy(bf16[128,3,128,128]{2,3,1,0:T(8,128)(2,1)} %bitcast.28) | data formatting | bytes 25165824 | tf_op jit(solution)/shard_map/reshape | solution.py:49
  78.2 0.0 all-to-all-done
  78.2 10.2 %all-to-all-start.1 = ((bf16[128,3,128,128]{3,2,1,0:T(8,128)(2,1)}), bf16[128,3,128,128]{3,2,1,0:T(8,128)(2,1)}, u32[]{:S(2)}, u32[]{:S(2)}) async-start(bf16[128,3,128,128]{3,2,1,0:T(8,128)(2,1)} %copy.36), calls=%async_computation.1 | async-start | bytes 25165824 | tf_op jit(solution)/shard_map/all_to_all | solution.py:48
  88.3 0.2 all-reduce.3.cloned.1.call-start
  88.6 0.0 copy-done
  88.6 0.0 copy-start.2
  88.6 0.0 copy-start.4
  88.6 3.1 fusion.3
  91.7 0.0 copy-done.2
  91.7 0.0 copy-done.4
  91.7 1.4 fusion.4
  93.1 0.0 all-reduce.3.cloned.1.call-update
  93.1 0.2 convert_reduce_fusion
  93.3 0.2 reshape.209
  93.5 247.9 %all-reduce.3.cloned.1.call-done = (f32[128,128]{0,1:T(8,128)}, f32[128,128]{0,1:T(8,128)}) async-done(((f32[128,128]{0,1:T(8,128)}, f32[128,128]{0,1:T(8,128)}), (f32[128,128]{0,1:T(8,128)}, f32[128,128]{0,1:T(8,128)})) %all-reduce.3.cloned.1.call-update) | async-done | bytes 131088 | tf_op jit(solution)/shard_map/psum | solution.py:84
  341.4 1.6 copy.39
  343.0 1.6 copy.40
  344.6 0.0 all-to-all-done.1
  344.6 13.6 %fusion = f32[64,128,128]{2,0,1:T(8,128)S(1)} fusion(bf16[384,128,128]{2,1,0:T(8,128)(2,1)} %bitcast.6, f32[384]{0:T(512)S(1)} %reshape.209), kind=kOutput, calls=%fused_computation.3 | convolution fusion | flops 805330944 | bytes 16778752 | tf_op jit(solution)/shard_map/bs,sjk->bjk/dot_general | solution.py:67
  358.1 0.0 copy-start.3
  358.1 0.0 copy-start.5
  358.2 2.4 copy.38
  360.6 0.0 copy-done.3
  360.6 0.0 copy-done.5
  360.6 2.0 fusion.2
  (5 shorter events, 0.1 us)
Async XLA Ops:
  7.2 81.4 %copy-start = (bf16[8192,128]{1,0:T(8,128)(2,1)S(1)}, bf16[8192,128]{1,0:T(8,128)(2,1)}, u32[]{:S(2)}) copy-start(bf16[8192,128]{1,0:T(8,128)(2,1)} %param.13) | copy-start | bytes 6291460
  9.1 69.1 %all-to-all-start = ((bf16[128,1,3]{2,1,0:T(2,128)(2,1)}), bf16[128,1,3]{2,1,0:T(2,128)(2,1)S(1)}, u32[]{:S(2)}, u32[]{:S(2)}) async-start(bf16[128,1,3]{2,1,0:T(2,128)(2,1)} %copy.34), calls=%async_computation | async-start | bytes 131072 | tf_op jit(solution)/shard_map/all_to_all | solution.py:55
  24.9 2.5 copy-start.6
  27.4 4.8 %copy-start.1 = (bf16[8192,128]{1,0:T(8,128)(2,1)}, bf16[8192,128]{1,0:T(8,128)(2,1)S(1)}, u32[]{:S(2)}) copy-start(bf16[8192,128]{1,0:T(8,128)(2,1)S(1)} %compare_select_fusion) | copy-start | bytes 6291460
  78.2 266.4 %all-to-all-start.1 = ((bf16[128,3,128,128]{3,2,1,0:T(8,128)(2,1)}), bf16[128,3,128,128]{3,2,1,0:T(8,128)(2,1)}, u32[]{:S(2)}, u32[]{:S(2)}) async-start(bf16[128,3,128,128]{3,2,1,0:T(8,128)(2,1)} %copy.36), calls=%async_computation.1 | async-start | bytes 25165824 | tf_op jit(solution)/shard_map/all_to_all | solution.py:48
  88.3 253.1 %all-reduce.3.cloned.1.call-start = ((), (), s32[]{:S(2)}) async-start(), calls=%async_computation.2 | async-start | bytes 262144 | tf_op jit(solution)/shard_map/psum | solution.py:84
  88.6 3.2 copy-start.2
  88.6 3.1 copy-start.4
  358.1 2.5 copy-start.3
  358.1 2.5 copy-start.5
Sparse Core Ops, SparseCore 0:
  94.7 246.7 all-reduce.2
where the time goes:
time: 372 us; the launch traced here: 369 us
  waiting for transfers between devices  248 us (67%)
  matrix products  41.4 us (11%)
  local copies, waits for them, and re-layouts  40.7 us (11%)
  starting transfers between devices  21.2 us (6%)
  between operations  14.2 us (4%)
  other arithmetic  4.2 us (1%)
    psum x1, waiting for transfers between devices, body(): lax.psum((local_self, local_neigh), ('gx', 'gy'))  248 us
    reshape x1, local copies, waits for them, and re-layouts, body(): outgoing.reshape(peer_count, capacity, block_size, feat_width)  16.6 us
    dot_general x1, matrix products, body(): jnp.einsum('sij,sik->sjk', tile_values, picked_rows, preferred_element_ty...  16.5 us
    dot_general x1, matrix products, body(): jnp.einsum('bs,sjk->bjk', one_hot, got_blocks, preferred_element_type=jnp...  13.6 us
    gather x1, local copies, waits for them, and re-layouts, body(): scaled_grad.reshape(blocks_dev, block_size, feat_width)  12.9 us
    all_to_all x1, starting transfers between devices, body(): lax.all_to_all(columns.reshape(peer_count, capacity), ('gx', 'gy'), split...  10.8 us
    all_to_all x1, starting transfers between devices, body(): lax.all_to_all(outgoing.reshape(peer_count, capacity, block_size, feat_wi...  10.2 us
  transfers between devices with their start and end apart: 3, of which 1 were waited for; matrix products, arithmetic and copies ran while one was open for 18% of the time, Pallas kernels for 0%

commit v1 on v0

v1 whole, which is shorter than its diff:
```python
import functools
import math

import jax
import jax.numpy as jnp
from jax import lax
from jax.experimental import pallas as pl
from jax.experimental.pallas import tpu as pltpu
from jax.sharding import PartitionSpec as P

BF16 = jnp.bfloat16
F32 = jnp.float32
AXES = ("gx", "gy")
NT = (((1,), (1,)), ((), ()))
TN = (((0,), (0,)), ((), ()))
VMEM_LIMIT = 50 * 1024 * 1024
EXTRA = 8


def dot(a, b, dims=(((1,), (0,)), ((), ()))):
    return lax.dot_general(a, b, dims, preferred_element_type=F32)


def params():
    return pltpu.CompilerParams(
        dimension_semantics=("arbitrary",), vmem_limit_bytes=VMEM_LIMIT
    )


def cost(flops, nbytes):
    return pl.CostEstimate(flops=flops, bytes_accessed=nbytes, transcendentals=0)


def relu_of(grad_ref, pre_ref):
    grad = grad_ref[...]
    return jnp.where(pre_ref[...] > 0, grad, jnp.zeros_like(grad))


def node_kernel(scale, grad_ref, pre_ref, feat_ref, mean_ref, wn_ref, deg_ref, gn_ref, st_ref, gw_ref):
    width = wn_ref.shape[0]
    blocks = st_ref.shape[0]
    relu = relu_of(grad_ref, pre_ref)
    relu_t = relu.T
    wn = wn_ref[...]
    gn_ref[...] = dot(relu, wn, NT).astype(BF16)
    ngt = dot(wn, relu_t)
    inv = 1.0 / deg_ref[...].astype(F32)
    block = deg_ref.shape[1]
    for b in range(blocks):
        st_ref[b] = (ngt[:, b * block : (b + 1) * block] * inv[b : b + 1, :]).astype(BF16)

    @pl.when(pl.program_id(0) == 0)
    def _():
        gw_ref[...] = jnp.zeros_like(gw_ref)

    gw_ref[:, :width] += dot(relu_t, feat_ref[...]) * scale
    gw_ref[:, width:] += dot(relu_t, mean_ref[...]) * scale


def node_stage(grad_out, preact, features, mean, w_neigh, degrees, block, scale):
    rows, width = grad_out.shape
    tile = 8 * block
    steps = rows // tile
    node = pl.BlockSpec((tile, width), lambda i: (i, 0))
    return pl.pallas_call(
        functools.partial(node_kernel, scale),
        grid=(steps,),
        in_specs=[
            node,
            node,
            node,
            node,
            pl.BlockSpec((width, width), lambda i: (0, 0)),
            pl.BlockSpec((8, block), lambda i: (i, 0)),
        ],
        out_specs=[
            node,
            pl.BlockSpec((8, width, block), lambda i: (i, 0, 0)),
            pl.BlockSpec((width, 2 * width), lambda i: (0, 0)),
        ],
        out_shape=[
            jax.ShapeDtypeStruct((rows, width), BF16),
            jax.ShapeDtypeStruct((rows // block, width, block), BF16),
            jax.ShapeDtypeStruct((width, 2 * width), F32),
        ],
        compiler_params=params(),
        cost_estimate=cost(8 * rows * width * width, 14 * rows * width),
        name="node_stage",
    )(grad_out, preact, features, mean, w_neigh, degrees.reshape(rows // block, block))


def hi_lo_rows(a, b, tail):
    width = a.shape[1]
    row = lax.broadcasted_iota(jnp.int32, (EXTRA, width), 0)
    a = jnp.broadcast_to(a, (EXTRA, width))
    b = jnp.broadcast_to(b, (EXTRA, width))
    a_hi = a.astype(BF16).astype(F32)
    b_hi = b.astype(BF16).astype(F32)
    out = jnp.where(row == 0, a_hi, jnp.where(row == 1, b_hi, jnp.where(row == 2, a - a_hi, b - b_hi)))
    return jnp.where(row < 4, out, jnp.where(row == 4, tail, 0.0))


def term_kernel(slots, capacity, group, transposed, list_ref, count_ref, st_ref, tile_ref, *rest):
    blocks = st_ref.shape[0]
    width = st_ref.shape[1]
    step = pl.program_id(0)
    *gw_ref, out_ref = rest
    if gw_ref:
        share = gw_ref[0][pl.ds(pl.multiple_of(step * group, group), group), :]
    for d in range(group):
        dest = step * group + d
        for k, slot in enumerate(slots):
            s = dest * capacity + slot
            row = lax.rem(list_ref[0, s], blocks)
            rows_t = st_ref[row]
            if transposed:
                term = dot(rows_t, tile_ref[d, k])
            else:
                term = dot(tile_ref[d, k], rows_t, (((0,), (1,)), ((), ())))
            keep = slot < count_ref[dest]
            out_ref[d, k * width : (k + 1) * width, :] = jnp.where(keep, term, 0.0).astype(BF16)
        base = len(slots) * width
        if gw_ref:
            lane = lax.broadcasted_iota(jnp.int32, (1, width), 1)
            cols = jnp.zeros((1, width), jnp.int32)
            for c in range(capacity):
                cols = jnp.where(lane == c, lax.rem(list_ref[1, dest * capacity + c], blocks), cols)
            a = share[d : d + 1, :width]
            b = share[d : d + 1, width:]
            extra = hi_lo_rows(a, b, jnp.broadcast_to(cols.astype(F32), (EXTRA, width)))
            out_ref[d, base : base + EXTRA, :] = extra.astype(BF16)
        else:
            out_ref[d, base : base + EXTRA, :] = jnp.zeros((EXTRA, width), BF16)


def terms(tile_list, counts, st, tiles, slots, transposed, gw=None, group=8):
    peers, capacity, block, _ = tiles.shape
    blocks, width, _ = st.shape
    n = len(slots)
    at = slots[0] // n
    rows = n * block + EXTRA
    in_specs = [
        pl.BlockSpec((blocks, width, block), lambda i, *_: (0, 0, 0)),
        pl.BlockSpec((group, n, block, block), lambda i, *_: (i, at, 0, 0)),
    ]
    args = [st, tiles]
    if gw is not None:
        in_specs.append(pl.BlockSpec(gw.shape, lambda i, *_: (0, 0)))
        args.append(gw)
    return pl.pallas_call(
        functools.partial(term_kernel, slots, capacity, group, transposed),
        grid_spec=pltpu.PrefetchScalarGridSpec(
            num_scalar_prefetch=2,
            grid=(peers // group,),
            in_specs=in_specs,
            out_specs=pl.BlockSpec((group, rows, width), lambda i, *_: (i, 0, 0)),
        ),
        out_shape=jax.ShapeDtypeStruct((peers, rows, width), BF16),
        compiler_params=params(),
        cost_estimate=cost(2 * peers * n * block**3, 4 * peers * n * block * block),
        name="terms",
    )(tile_list, counts, *args)


def first_sum_kernel(group, cols_ref, got_ref, grad_ref, pre_ref, ws_ref, out_ref, acc):
    step = pl.program_id(0)
    steps = pl.num_programs(0)
    block = acc.shape[1]

    @pl.when(step == 0)
    def _():
        acc[...] = jnp.zeros_like(acc)

    for d in range(group):
        col = cols_ref[2, step * group + d]
        acc[col] += got_ref[d, :block, :].astype(F32)

    @pl.when(step == steps - 1)
    def _():
        @pl.loop(0, acc.shape[0])
        def _(b):
            at = pl.ds(pl.multiple_of(b * block, block), block)
            relu = relu_of(grad_ref.at[at], pre_ref.at[at])
            out_ref[b] = acc[b].T + dot(relu, ws_ref[...], NT)


def first_sum(cols, got, grad_out, preact, w_self, group=8):
    peers, rows, width = got.shape
    nodes = grad_out.shape[0]
    block = rows - EXTRA
    blocks = nodes // block
    whole = pl.BlockSpec((nodes, width), lambda i, *_: (0, 0))
    return pl.pallas_call(
        functools.partial(first_sum_kernel, group),
        grid_spec=pltpu.PrefetchScalarGridSpec(
            num_scalar_prefetch=1,
            grid=(peers // group,),
            in_specs=[
                pl.BlockSpec((group, rows, width), lambda i, *_: (i, 0, 0)),
                whole,
                whole,
                pl.BlockSpec((width, width), lambda i, *_: (0, 0)),
            ],
            out_specs=pl.BlockSpec((blocks, block, width), lambda i, *_: (0, 0, 0)),
            scratch_shapes=[pltpu.VMEM((blocks, block, width), F32)],
        ),
        out_shape=jax.ShapeDtypeStruct((blocks, block, width), F32),
        compiler_params=params(),
        cost_estimate=cost(2 * nodes * width * width, 2 * peers * rows * width + 8 * nodes * width),
        name="first_sum",
    )(cols, got, grad_out, preact, w_self)


def last_sum_kernel(group, slots, cols_ref, got_ref, base_ref, out_ref, gs_ref, gn_ref, acc, gw, sem):
    step = pl.program_id(0)
    steps = pl.num_programs(0)
    block, width = acc.shape[1:]
    load = pltpu.make_async_copy(base_ref, acc, sem)

    @pl.when(step == 0)
    def _():
        load.start()
        load.wait()

    shares = []
    for d in range(group):
        src = step * group + d
        for k in range(slots):
            col = cols_ref[k, src]
            acc[col] += got_ref[d, k * block : (k + 1) * block, :].astype(F32)
        extra = got_ref[d, slots * block : slots * block + EXTRA, :].astype(F32)
        shares.append(extra[:2] + extra[2:4])
    at = pl.ds(pl.multiple_of(step * group, group), group)
    gw[at, :width] = jnp.concatenate([share[:1] for share in shares], axis=0)
    gw[at, width:] = jnp.concatenate([share[1:] for share in shares], axis=0)

    @pl.when(step == steps - 1)
    def _():
        @pl.loop(0, acc.shape[0])
        def _(b):
            out_ref[b] = acc[b].astype(BF16)

        gs_ref[...] = gw[:, :width].T
        gn_ref[...] = gw[:, width:].T


def last_sum(cols, got, base, slots, group=8):
    peers, rows, width = got.shape
    blocks, block, _ = base.shape
    square = pl.BlockSpec((width, width), lambda i, *_: (0, 0))
    return pl.pallas_call(
        functools.partial(last_sum_kernel, group, slots),
        grid_spec=pltpu.PrefetchScalarGridSpec(
            num_scalar_prefetch=1,
            grid=(peers // group,),
            in_specs=[
                pl.BlockSpec((group, rows, width), lambda i, *_: (i, 0, 0)),
                pl.BlockSpec(memory_space=pl.ANY),
            ],
            out_specs=[
                pl.BlockSpec((blocks, block, width), lambda i, *_: (0, 0, 0)),
                square,
                square,
            ],
            scratch_shapes=[
                pltpu.VMEM((blocks, block, width), F32),
                pltpu.VMEM((width, 2 * width), F32),
                pltpu.SemaphoreType.DMA,
            ],
        ),
        out_shape=[
            jax.ShapeDtypeStruct((blocks, block, width), BF16),
            jax.ShapeDtypeStruct((width, width), F32),
            jax.ShapeDtypeStruct((width, width), F32),
        ],
        compiler_params=params(),
        cost_estimate=cost(peers * rows * width, 2 * peers * rows * width + 6 * blocks * block * width),
        name="last_sum",
    )(cols, got, base)


def exchange(x):
    return lax.all_to_all(x, AXES, split_axis=0, concat_axis=0, tiled=True)


def body(
    grad_out,
    preact,
    features,
    neighbour_mean,
    w_self,
    w_neigh,
    degrees,
    tile_values,
    tile_list,
    send_counts,
):
    nodes, width = grad_out.shape
    block = tile_values.shape[1]
    peers = lax.axis_size("gx") * lax.axis_size("gy")
    capacity = tile_values.shape[0] // peers
    scale = 1.0 / math.sqrt(nodes * peers)
    slot_list = tile_list[0]
    counts = send_counts[0]
    tiles = tile_values.reshape(peers, capacity, block, block)
    last = capacity - 1

    grad_neighbour, st, gw = node_stage(
        grad_out, preact, features, neighbour_mean, w_neigh, degrees, block, scale
    )
    sent1 = terms(slot_list, counts, st, tiles, (last,), True, gw)
    got1 = exchange(sent1)
    sent2 = terms(slot_list, counts, st, tiles, tuple(range(last)), False)

    extra = got1[:, block : block + EXTRA, :]
    share = jnp.sum(extra[:, :4, :].astype(F32), axis=0)
    share = share[:2] + share[2:]
    high = share.astype(BF16)
    low = (share - high.astype(F32)).astype(BF16)
    pay = jnp.concatenate([high, low, jnp.zeros((EXTRA - 4, width), BF16)], axis=0)
    sent2 = lax.dynamic_update_slice(
        sent2, jnp.broadcast_to(pay[None], (peers, EXTRA, width)), (0, last * block, 0)
    )
    got2 = exchange(sent2)
    cols = extra[:, 4, :8].astype(jnp.int32).T
    base = first_sum(cols, got1, grad_out, preact, w_self)
    grad_features, grad_w_self, grad_w_neigh = last_sum(cols, got2, base, last)
    return (grad_features.reshape(nodes, width), grad_neighbour, grad_w_self, grad_w_neigh)


def solution(mesh):
    placed = (
        P(AXES, None),
        P(AXES, None),
        P(AXES, None),
        P(AXES, None),
        P(),
        P(),
        P(AXES),
        P(AXES, None, None),
        P(AXES, None, None),
        P(AXES, None),
    )
    return jax.shard_map(
        body,
        mesh=mesh,
        in_specs=placed,
        out_specs=(P(AXES, None), P(AXES, None), P(), P()),
        check_vma=False,
    )
```

time: 372 us -> 223 us (0.60)
  waiting for transfers between devices: 248 us -> 125 us
  Pallas kernels: 0 us -> 74 us
  matrix products: 41.4 us -> 0 us
  local copies, waits for them, and re-layouts: 40.7 us -> 3.48 us
  between operations: 14.2 us -> 0.7 us
  starting transfers between devices: 21.2 us -> 17.2 us
    psum x1 -> x0, waiting for transfers between devices: 248 us -> none  [body(): lax.psum((local_self, local_neigh), ('gx', 'gy'))]
    all_to_all x2, waiting for transfers between devices: 0.01 us -> 125 us  [exchange(): return lax.all_to_all(x, AXES, split_axis=0, concat_axis=0, tiled=True)]
    pallas_call x0 -> x5, Pallas kernels: none -> 74 us  [the longest x2 28.6 us: terms(): pl.pallas_call(functools.partial(term_kernel, slots, capacity, group, tra...]
    dot_general x6 -> x0, matrix products: 41.4 us -> none  [the longest x1 16.5 us: body(): jnp.einsum('sij,sik->sjk', tile_values, picked_rows, preferred_element_ty...]
    reshape x1 -> x0, local copies, waits for them, and re-layouts: 16.6 us -> none  [body(): outgoing.reshape(peer_count, capacity, block_size, feat_width)]
    gather x2 -> x0, local copies, waits for them, and re-layouts: 16.4 us -> none  [the longest x1 12.9 us: body(): scaled_grad.reshape(blocks_dev, block_size, feat_width)]
    all_to_all x2, starting transfers between devices: 20.9 us -> 17.2 us  [exchange(): return lax.all_to_all(x, AXES, split_axis=0, concat_axis=0, tiled=True)]
  transfers between devices with their start and end apart: 3 -> 2, of which waited for: 1 -> 2; matrix products, arithmetic and copies ran while one was open for 18% -> 1% of each run, Pallas kernels for 0% -> 17%
where the time goes in v1:
time: 223 us; the launch traced here: 221 us
  waiting for transfers between devices  125 us (56%)
  Pallas kernels  74 us (33%)
  starting transfers between devices  17.2 us (8%)
  local copies, waits for them, and re-layouts  3.48 us (2%)
    all_to_all x2, waiting for transfers between devices, exchange(): return lax.all_to_all(x, AXES, split_axis=0, concat_axis=0, tiled=True)  125 us
    pallas_call x2, Pallas kernels, terms(): pl.pallas_call(functools.partial(term_kernel, slots, capacity, group, tra...  28.6 us
    pallas_call x1, Pallas kernels, first_sum(): pl.pallas_call(functools.partial(first_sum_kernel, group), grid_spec=pltp...  22 us
    all_to_all x2, starting transfers between devices, exchange(): return lax.all_to_all(x, AXES, split_axis=0, concat_axis=0, tiled=True)  17.2 us
    pallas_call x1, Pallas kernels, last_sum(): pl.pallas_call(functools.partial(last_sum_kernel, group, slots), grid_spe...  14.7 us
    pallas_call x1, Pallas kernels, node_stage(): pl.pallas_call(functools.partial(node_kernel, scale), grid=(steps,), in_s...  8.66 us
  transfers between devices with their start and end apart: 2, of which 2 were waited for; matrix products, arithmetic and copies ran while one was open for 1% of the time, Pallas kernels for 17%

profile of v1, /device:TPU:7, one launch (start us, length us, event | category | flops | bytes accessed | tf_op | source)
XLA Modules:
  0.0 221.4 jit_solution(10730697852708273805)
XLA Ops:
  0.6 0.0 copy-start.5
  0.6 0.0 copy-start.1
  0.7 0.8 copy-done.1
  1.4 0.0 copy-start.2
  1.4 0.8 copy-done.2
  2.2 0.0 copy-start.4
  2.2 8.7 %node_stage.1 = (bf16[8192,128]{1,0:T(8,128)(2,1)}, bf16[64,128,128]{2,1,0:T(8,128)(2,1)S(1)}, f32[128,256]{1,0:T(8,128)S(1)}) custom-call(bf16[8192,128]{1,0:T(8,128)(2,1)} %grad_ref.3, bf16[8192,128]{1,0:T(8,128)(2,1)} %pre_ref.3, bf16[8192,128]{1,0:T(8,128)(2,1)} %feat_ref.1, bf16[8192,128]{1,0:T(8,128)(2,1)} %mean_ref.1, bf16[128,128]{1,0:T(8,128)(2,1)S(1)} %copy-done.1, ...), custom_call_target="tpu_custom_call" | custom-call | flops 1073741824 | bytes 14680064 | tf_op jit(solution)/shard_map/node_stage/pallas_call | solution.py:65
  10.8 0.0 copy-done.5
  10.8 0.0 copy-done.4
  10.8 12.5 %terms.2 = bf16[128,136,128]{2,1,0:T(8,128)(2,1)} custom-call(s32[2,384]{1,0:T(2,128)S(1)} %bitcast.11, s32[128]{0:T(128)S(1)} %bitcast.13, bf16[64,128,128]{2,1,0:T(8,128)(2,1)S(1)} %get-tuple-element.10.st_ref, bf16[128,3,128,128]{3,2,1,0:T(8,128)(2,1)} %bitcast.15, f32[128,256]{1,0:T(8,128)S(1)} %get-tuple-element.11.rest_0_), custom_call_target="tpu_custom_call" | custom-call | flops 536870912 | bytes 8388608 | tf_op jit(solution)/shard_map/terms/pallas_call | solution.py:150
  23.3 11.2 %all-to-all-start = ((bf16[128,136,128]{2,1,0:T(8,128)(2,1)}), bf16[128,136,128]{2,1,0:T(8,128)(2,1)}, u32[]{:S(2)}, u32[]{:S(2)}) async-start(bf16[128,136,128]{2,1,0:T(8,128)(2,1)} %terms.2), calls=%async_computation | async-start | bytes 8912896 | tf_op jit(solution)/shard_map/all_to_all | solution.py:283
  34.5 0.1 pad.2.clone
  34.6 16.1 %terms.3 = bf16[128,264,128]{2,1,0:T(8,128)(2,1)} custom-call(s32[2,384]{1,0:T(2,128)S(1)} %bitcast.12, s32[128]{0:T(128)S(1)} %bitcast.14, bf16[64,128,128]{2,1,0:T(8,128)(2,1)S(1)} %get-tuple-element.10.st_ref, bf16[128,3,128,128]{3,2,1,0:T(8,128)(2,1)} %bitcast.16), custom_call_target="tpu_custom_call" | custom-call | flops 1073741824 | bytes 16777216 | tf_op jit(solution)/shard_map/terms/pallas_call | solution.py:150
  50.7 37.6 %all-to-all-done.got_ref = bf16[128,136,128]{2,1,0:T(8,128)(2,1)} async-done(((bf16[128,136,128]{2,1,0:T(8,128)(2,1)}), bf16[128,136,128]{2,1,0:T(8,128)(2,1)}, u32[]{:S(2)}, u32[]{:S(2)}) %all-to-all-start) | async-done | bytes 4456480 | tf_op jit(solution)/shard_map/all_to_all | solution.py:283
  88.3 1.1 convert_reduce_fusion
  89.4 0.1 maximum_maximum_fusion
  89.5 0.8 broadcast_dynamic-update-slice_fusion
  90.3 0.0 copy-start
  90.3 0.0 copy-start.3
  90.3 6.0 %all-to-all-start.1 = ((bf16[128,264,128]{2,1,0:T(8,128)(2,1)}), bf16[128,264,128]{2,1,0:T(8,128)(2,1)}, u32[]{:S(2)}, u32[]{:S(2)}) async-start(bf16[128,264,128]{2,1,0:T(8,128)(2,1)} %broadcast_dynamic-update-slice_fusion), calls=%async_computation.1 | async-start | bytes 17301504 | tf_op jit(solution)/shard_map/all_to_all | solution.py:283
  96.3 1.0 slice.19
  97.3 0.1 copy.17
  97.4 0.0 copy-done
  97.4 0.0 copy-done.3
  97.4 22.0 %first_sum.1.base_ref = f32[64,128,128]{2,1,0:T(8,128)} custom-call(s32[8,128]{1,0:T(8,128)S(1)} %convert_bitcast_fusion.cols_ref, bf16[128,136,128]{2,1,0:T(8,128)(2,1)} %all-to-all-done.got_ref, bf16[8192,128]{1,0:T(8,128)(2,1)S(1)} %copy-done, bf16[8192,128]{1,0:T(8,128)(2,1)} %pre_ref.3, bf16[128,128]{1,0:T(8,128)(2,1)S(1)} %copy-done.3), custom_call_target="tpu_custom_call" | custom-call | flops 268435456 | bytes 12845056 | tf_op jit(solution)/shard_map/first_sum/pallas_call | solution.py:193
  119.5 87.2 %all-to-all-done.1.got_ref = bf16[128,264,128]{2,1,0:T(8,128)(2,1)} async-done(((bf16[128,264,128]{2,1,0:T(8,128)(2,1)}), bf16[128,264,128]{2,1,0:T(8,128)(2,1)}, u32[]{:S(2)}, u32[]{:S(2)}) %all-to-all-start.1) | async-done | bytes 8650784 | tf_op jit(solution)/shard_map/all_to_all | solution.py:283
  206.6 14.7 %last_sum.1 = (bf16[64,128,128]{2,1,0:T(8,128)(2,1)}, f32[128,128]{1,0:T(8,128)}, f32[128,128]{1,0:T(8,128)}) custom-call(s32[8,128]{1,0:T(8,128)S(1)} %convert_bitcast_fusion.cols_ref, bf16[128,264,128]{2,1,0:T(8,128)(2,1)} %all-to-all-done.1.got_ref, f32[64,128,128]{2,1,0:T(8,128)} %first_sum.1.base_ref), custom_call_target="tpu_custom_call" | custom-call | flops 4325376 | bytes 14942208 | tf_op jit(solution)/shard_map/last_sum/pallas_call | solution.py:251
  (3 shorter events, 0.0 us)
Async XLA Ops:
  0.6 10.2 %copy-start.5 = (s32[1,128]{1,0:T(1,128)S(1)}, s32[1,128]{1,0:T(1,128)}, u32[]{:S(2)}) copy-start(s32[1,128]{1,0:T(1,128)} %param.19) | copy-start | bytes 1540
  0.6 0.8 copy-start.1
  1.4 0.8 copy-start.2
  2.2 8.7 %copy-start.4 = (s32[1,2,384]{2,1,0:T(2,128)S(1)}, s32[1,2,384]{2,1,0:T(2,128)}, u32[]{:S(2)}) copy-start(s32[1,2,384]{2,1,0:T(2,128)} %param.18) | copy-start | bytes 9220
  23.3 65.1 %all-to-all-start = ((bf16[128,136,128]{2,1,0:T(8,128)(2,1)}), bf16[128,136,128]{2,1,0:T(8,128)(2,1)}, u32[]{:S(2)}, u32[]{:S(2)}) async-start(bf16[128,136,128]{2,1,0:T(8,128)(2,1)} %terms.2), calls=%async_computation | async-start | bytes 8912896 | tf_op jit(solution)/shard_map/all_to_all | solution.py:283
  90.3 7.1 %copy-start = (bf16[8192,128]{1,0:T(8,128)(2,1)S(1)}, bf16[8192,128]{1,0:T(8,128)(2,1)}, u32[]{:S(2)}) copy-start(bf16[8192,128]{1,0:T(8,128)(2,1)} %grad_ref.3) | copy-start | bytes 6291460
  90.3 7.1 %copy-start.3 = (bf16[128,128]{1,0:T(8,128)(2,1)S(1)}, bf16[128,128]{1,0:T(8,128)(2,1)}, u32[]{:S(2)}) copy-start(bf16[128,128]{1,0:T(8,128)(2,1)} %ws_ref.1) | copy-start | bytes 98308
  90.3 116.3 %all-to-all-start.1 = ((bf16[128,264,128]{2,1,0:T(8,128)(2,1)}), bf16[128,264,128]{2,1,0:T(8,128)(2,1)}, u32[]{:S(2)}, u32[]{:S(2)}) async-start(bf16[128,264,128]{2,1,0:T(8,128)(2,1)} %broadcast_dynamic-update-slice_fusion), calls=%async_computation.1 | async-start | bytes 17301504 | tf_op jit(solution)/shard_map/all_to_all | solution.py:283

commit v2 on v1

v2 whole, which is shorter than its diff:
```python
import functools
import math

import jax
import jax.numpy as jnp
from jax import lax
from jax.experimental import pallas as pl
from jax.experimental.pallas import tpu as pltpu
from jax.sharding import PartitionSpec as P

BF16 = jnp.bfloat16
F32 = jnp.float32
AXES = ("gx", "gy")
NT = (((1,), (1,)), ((), ()))
TN = (((0,), (0,)), ((), ()))
VMEM_LIMIT = 50 * 1024 * 1024
FULL_VMEM = 60 * 1024 * 1024
EXTRA = 8


def dot(a, b, dims=(((1,), (0,)), ((), ()))):
    return lax.dot_general(a, b, dims, preferred_element_type=F32)


def params():
    return pltpu.CompilerParams(
        dimension_semantics=("arbitrary",), vmem_limit_bytes=VMEM_LIMIT
    )


def cost(flops, nbytes):
    return pl.CostEstimate(flops=flops, bytes_accessed=nbytes, transcendentals=0)


def local(index, blocks):
    return index & (blocks - 1) if blocks & (blocks - 1) == 0 else lax.rem(index, blocks)


def relu_of(grad_ref, pre_ref):
    grad = grad_ref[...]
    return jnp.where(pre_ref[...] > 0, grad, jnp.zeros_like(grad))


def scaled_rows(wn, relu_t, deg, st_ref, at):
    block = deg.shape[1]
    ngt = dot(wn, relu_t)
    inv = 1.0 / deg.astype(F32)
    for b in range(deg.shape[0]):
        st_ref[at + b] = (ngt[:, b * block : (b + 1) * block] * inv[b : b + 1, :]).astype(BF16)


def node_kernel(grad_ref, pre_ref, wn_ref, deg_ref, gn_ref, st_ref):
    relu = relu_of(grad_ref, pre_ref)
    wn = wn_ref[...]
    gn_ref[...] = dot(relu, wn, NT).astype(BF16)
    scaled_rows(wn, relu.T, deg_ref[...], st_ref, 0)


def node_stage(grad_out, preact, w_neigh, degrees):
    rows, width = grad_out.shape
    blocks, block = degrees.shape
    tile = 8 * block
    node = pl.BlockSpec((tile, width), lambda i: (i, 0))
    return pl.pallas_call(
        node_kernel,
        grid=(rows // tile,),
        in_specs=[
            node,
            node,
            pl.BlockSpec((width, width), lambda i: (0, 0)),
            pl.BlockSpec((8, block), lambda i: (i, 0)),
        ],
        out_specs=[node, pl.BlockSpec((8, width, block), lambda i: (i, 0, 0))],
        out_shape=[
            jax.ShapeDtypeStruct((rows, width), BF16),
            jax.ShapeDtypeStruct((blocks, width, block), BF16),
        ],
        compiler_params=params(),
        cost_estimate=cost(4 * rows * width * width, 8 * rows * width),
        name="node_stage",
    )(grad_out, preact, w_neigh, degrees)


def hi_lo_rows(a, b, tail):
    width = a.shape[1]
    row = lax.broadcasted_iota(jnp.int32, (EXTRA, width), 0)
    a = jnp.broadcast_to(a, (EXTRA, width))
    b = jnp.broadcast_to(b, (EXTRA, width))
    a_hi = a.astype(BF16).astype(F32)
    b_hi = b.astype(BF16).astype(F32)
    out = jnp.where(row == 0, a_hi, jnp.where(row == 1, b_hi, jnp.where(row == 2, a - a_hi, b - b_hi)))
    return jnp.where(row < 4, out, jnp.where(row == 4, tail, 0.0))


def term_rows(slots, capacity, group, step, list_ref, count_ref, st_ref, tile_ref, out_ref, at, transposed, share):
    blocks, width, _ = st_ref.shape
    base = len(slots) * width
    for d in range(group):
        dest = step * group + d
        for k, slot in enumerate(slots):
            rows_t = st_ref[local(list_ref[0, dest * capacity + slot], blocks)]
            if transposed:
                term = dot(rows_t, tile_ref[at + d, k])
            else:
                term = dot(tile_ref[at + d, k], rows_t, (((0,), (1,)), ((), ())))
            keep = slot < count_ref[0, dest]
            out_ref[at + d, k * width : (k + 1) * width, :] = jnp.where(keep, term, 0.0).astype(BF16)
        if share is None:
            extra = jnp.zeros((EXTRA, width), BF16)
        else:
            lane = lax.broadcasted_iota(jnp.int32, (1, width), 1)
            cols = jnp.zeros((1, width), jnp.int32)
            for c in range(capacity):
                cols = jnp.where(lane == c, local(list_ref[1, dest * capacity + c], blocks), cols)
            extra = hi_lo_rows(
                share[d : d + 1, :width],
                share[d : d + 1, width:],
                jnp.broadcast_to(cols.astype(F32), (EXTRA, width)),
            ).astype(BF16)
        out_ref[at + d, base : base + EXTRA, :] = extra


def term_kernel(slots, capacity, group, list_ref, count_ref, st_ref, tile_ref, out_ref):
    step = pl.program_id(0)
    term_rows(slots, capacity, group, step, list_ref, count_ref, st_ref, tile_ref, out_ref, 0, False, None)


def terms(tile_list, counts, st, tiles, slots, group=16):
    peers, capacity, block, _ = tiles.shape
    blocks, width, _ = st.shape
    n = len(slots)
    at = slots[0] // n
    rows = n * block + EXTRA
    return pl.pallas_call(
        functools.partial(term_kernel, slots, capacity, group),
        grid_spec=pltpu.PrefetchScalarGridSpec(
            num_scalar_prefetch=2,
            grid=(peers // group,),
            in_specs=[
                pl.BlockSpec((blocks, width, block), lambda i, *_: (0, 0, 0)),
                pl.BlockSpec((group, n, block, block), lambda i, *_: (i, at, 0, 0)),
            ],
            out_specs=pl.BlockSpec((group, rows, width), lambda i, *_: (i, 0, 0)),
        ),
        out_shape=jax.ShapeDtypeStruct((peers, rows, width), BF16),
        compiler_params=params(),
        cost_estimate=cost(2 * peers * n * block**3, 4 * peers * n * block * block),
        name="terms",
    )(tile_list, counts, st, tiles)


def first_kernel(
    scale, slot, chunks, groups,
    list_hbm, count_hbm, deg_hbm, wn_hbm, grad_hbm, pre_hbm, feat_hbm, mean_hbm, tile_hbm,
    out_hbm,
    list_ref, count_ref, deg_ref, wn_ref, grad_ref, pre_ref, feat_ref, mean_ref, tile_ref, out_ref, st_ref, gw_ref,
    small_sem, node_sem, tile_sem, out_sem,
):
    nodes, width = grad_ref.shape
    peers, capacity = tile_hbm.shape[:2]
    part = nodes // chunks
    group = peers // groups
    small = [
        pltpu.make_async_copy(src, dst, small_sem.at[i])
        for i, (src, dst) in enumerate(
            ((wn_hbm, wn_ref), (deg_hbm, deg_ref), (list_hbm, list_ref), (count_hbm, count_ref))
        )
    ]
    pairs = ((grad_hbm, grad_ref), (pre_hbm, pre_ref), (feat_hbm, feat_ref), (mean_hbm, mean_ref))

    def node_copies(c):
        at = pl.ds(pl.multiple_of(c * part, part), part)
        return [
            pltpu.make_async_copy(src.at[at], dst.at[at], node_sem.at[i, c])
            for i, (src, dst) in enumerate(pairs)
        ]

    def tile_copy(g):
        at = pl.ds(g * group, group)
        return pltpu.make_async_copy(tile_hbm.at[at, slot : slot + 1], tile_ref.at[at], tile_sem.at[g])

    def out_copy(g):
        at = pl.ds(g * group, group)
        return pltpu.make_async_copy(out_ref.at[at], out_hbm.at[at], out_sem.at[g])

    for copy in small[:2]:
        copy.start()
    for c in range(chunks):
        for copy in node_copies(c):
            copy.start()
    for copy in small[2:]:
        copy.start()
    for g in range(groups):
        tile_copy(g).start()
    gw_ref[...] = jnp.zeros_like(gw_ref)
    for copy in small[:2]:
        copy.wait()

    @pl.loop(0, chunks)
    def _(c):
        for copy in node_copies(c):
            copy.wait()
        at = pl.ds(pl.multiple_of(c * part, part), part)
        relu_t = relu_of(grad_ref.at[at], pre_ref.at[at]).T
        rows = part // deg_ref.shape[1]
        deg = deg_ref[pl.ds(pl.multiple_of(c * rows, rows), rows), :]
        scaled_rows(wn_ref[...], relu_t, deg, st_ref, c * rows)
        gw_ref[:, :width] += dot(relu_t, feat_ref[at, :]) * scale
        gw_ref[:, width:] += dot(relu_t, mean_ref[at, :]) * scale

    for copy in small[2:]:
        copy.wait()

    @pl.loop(0, groups)
    def _(g):
        tile_copy(g).wait()
        share = gw_ref[pl.ds(pl.multiple_of(g * group, group), group), :]
        term_rows(
            (slot,), capacity, group, g, list_ref, count_ref, st_ref,
            tile_ref, out_ref, g * group, True, share,
        )
        out_copy(g).start()

    for g in range(groups):
        out_copy(g).wait()


def first_stage(tile_list, counts, degrees, w_neigh, grad_out, preact, features, mean, tiles, slot, scale, chunks=4, groups=4):
    nodes, width = grad_out.shape
    peers, capacity, block, _ = tiles.shape
    blocks = nodes // block
    rows = block + EXTRA
    hbm = pl.BlockSpec(memory_space=pl.ANY)
    node = pltpu.VMEM((nodes, width), BF16)
    return pl.pallas_call(
        functools.partial(first_kernel, scale, slot, chunks, groups),
        in_specs=[hbm] * 9,
        out_specs=hbm,
        out_shape=jax.ShapeDtypeStruct((peers, rows, width), BF16),
        scratch_shapes=[
            pltpu.SMEM(tile_list.shape, jnp.int32),
            pltpu.SMEM(counts.shape, jnp.int32),
            pltpu.VMEM(degrees.shape, jnp.int32),
            pltpu.VMEM(w_neigh.shape, BF16),
            node,
            node,
            node,
            node,
            pltpu.VMEM((peers, 1, block, block), BF16),
            pltpu.VMEM((peers, rows, width), BF16),
            pltpu.VMEM((blocks, width, block), BF16),
            pltpu.VMEM((width, 2 * width), F32),
            pltpu.SemaphoreType.DMA((4,)),
            pltpu.SemaphoreType.DMA((4, chunks)),
            pltpu.SemaphoreType.DMA((groups,)),
            pltpu.SemaphoreType.DMA((groups,)),
        ],
        compiler_params=pltpu.CompilerParams(vmem_limit_bytes=FULL_VMEM),
        cost_estimate=cost(6 * nodes * width * width + 2 * peers * block**3, 8 * nodes * width + 4 * peers * block * block),
        name="first_stage",
    )(tile_list, counts, degrees, w_neigh, grad_out, preact, features, mean, tiles)


def first_sum_kernel(group, cols_ref, got_ref, grad_ref, pre_ref, ws_ref, out_ref, acc):
    step = pl.program_id(0)
    steps = pl.num_programs(0)
    block = acc.shape[1]

    @pl.when(step == 0)
    def _():
        acc[...] = jnp.zeros_like(acc)

    for d in range(group):
        col = cols_ref[2, step * group + d]
        acc[col] += got_ref[d, :block, :].astype(F32)

    @pl.when(step == steps - 1)
    def _():
        @pl.loop(0, acc.shape[0])
        def _(b):
            at = pl.ds(pl.multiple_of(b * block, block), block)
            relu = relu_of(grad_ref.at[at], pre_ref.at[at])
            out_ref[b] = acc[b].T + dot(relu, ws_ref[...], NT)


def first_sum(cols, got, grad_out, preact, w_self, group=8):
    peers, rows, width = got.shape
    nodes = grad_out.shape[0]
    block = rows - EXTRA
    blocks = nodes // block
    whole = pl.BlockSpec((nodes, width), lambda i, *_: (0, 0))
    return pl.pallas_call(
        functools.partial(first_sum_kernel, group),
        grid_spec=pltpu.PrefetchScalarGridSpec(
            num_scalar_prefetch=1,
            grid=(peers // group,),
            in_specs=[
                pl.BlockSpec((group, rows, width), lambda i, *_: (i, 0, 0)),
                whole,
                whole,
                pl.BlockSpec((width, width), lambda i, *_: (0, 0)),
            ],
            out_specs=pl.BlockSpec((blocks, block, width), lambda i, *_: (0, 0, 0)),
            scratch_shapes=[pltpu.VMEM((blocks, block, width), F32)],
        ),
        out_shape=jax.ShapeDtypeStruct((blocks, block, width), F32),
        compiler_params=params(),
        cost_estimate=cost(2 * nodes * width * width, 2 * peers * rows * width + 8 * nodes * width),
        name="first_sum",
    )(cols, got, grad_out, preact, w_self)


def last_sum_kernel(
    slots, groups, parts, cols_ref, got_hbm, base_hbm, out_hbm, gs_ref, gn_ref,
    got, out, acc, gw, got_sem, base_sem, out_sem,
):
    peers = got.shape[0]
    blocks, block, width = acc.shape[1:]
    group = peers // groups
    part = blocks // parts

    def got_copy(g):
        at = pl.ds(g * group, group)
        return pltpu.make_async_copy(got_hbm.at[at], got.at[at], got_sem.at[g])

    def out_copy(p):
        at = pl.ds(p * part, part)
        return pltpu.make_async_copy(out.at[at], out_hbm.at[at], out_sem.at[p])

    load = pltpu.make_async_copy(base_hbm, acc.at[0], base_sem)
    load.start()
    for g in range(groups):
        got_copy(g).start()

    for k in range(1, slots):
        @pl.loop(0, blocks, unroll=4)
        def _(b):
            acc[k, b] = jnp.zeros((block, width), F32)

    load.wait()

    @pl.loop(0, groups)
    def _(g):
        got_copy(g).wait()
        for d8 in range(0, group, 8):
            shares = []
            for d in range(d8, d8 + 8):
                src = g * group + d
                for k in range(slots):
                    col = cols_ref[k, src]
                    acc[k, col] += got[src, k * block : (k + 1) * block, :].astype(F32)
                extra = got[src, slots * block : slots * block + EXTRA, :].astype(F32)
                shares.append(extra[:2] + extra[2:4])
            at = pl.ds(pl.multiple_of(g * group + d8, 8), 8)
            gw[at, :width] = jnp.concatenate([share[:1] for share in shares], axis=0)
            gw[at, width:] = jnp.concatenate([share[1:] for share in shares], axis=0)

    @pl.loop(0, parts)
    def _(p):
        for b in range(part):
            total = acc[0, p * part + b]
            for k in range(1, slots):
                total += acc[k, p * part + b]
            out[p * part + b] = total.astype(BF16)
        out_copy(p).start()

    gs_ref[...] = gw[:, :width].T
    gn_ref[...] = gw[:, width:].T
    for p in range(parts):
        out_copy(p).wait()


def last_sum(cols, got, base, slots, groups=4, parts=4):
    peers, rows, width = got.shape
    blocks, block, _ = base.shape
    hbm = pl.BlockSpec(memory_space=pl.ANY)
    vmem = pl.BlockSpec(memory_space=pltpu.VMEM)
    return pl.pallas_call(
        functools.partial(last_sum_kernel, slots, groups, parts),
        in_specs=[pl.BlockSpec(memory_space=pltpu.SMEM), hbm, hbm],
        out_specs=[hbm, vmem, vmem],
        scratch_shapes=[
            pltpu.VMEM((peers, rows, width), BF16),
            pltpu.VMEM((blocks, block, width), BF16),
            pltpu.VMEM((slots, blocks, block, width), F32),
            pltpu.VMEM((width, 2 * width), F32),
            pltpu.SemaphoreType.DMA((groups,)),
            pltpu.SemaphoreType.DMA,
            pltpu.SemaphoreType.DMA((parts,)),
        ],
        out_shape=[
            jax.ShapeDtypeStruct((blocks, block, width), BF16),
            jax.ShapeDtypeStruct((width, width), F32),
            jax.ShapeDtypeStruct((width, width), F32),
        ],
        compiler_params=pltpu.CompilerParams(vmem_limit_bytes=FULL_VMEM),
        cost_estimate=cost(peers * rows * width, 2 * peers * rows * width + 6 * blocks * block * width),
        name="last_sum",
    )(cols, got, base)


def exchange(x):
    return lax.all_to_all(x, AXES, split_axis=0, concat_axis=0, tiled=True)


def body(
    grad_out,
    preact,
    features,
    neighbour_mean,
    w_self,
    w_neigh,
    degrees,
    tile_values,
    tile_list,
    send_counts,
):
    nodes, width = grad_out.shape
    block = tile_values.shape[1]
    peers = lax.axis_size("gx") * lax.axis_size("gy")
    capacity = tile_values.shape[0] // peers
    scale = 1.0 / math.sqrt(nodes * peers)
    slot_list = tile_list[0]
    tiles = tile_values.reshape(peers, capacity, block, block)
    last = capacity - 1

    degrees = degrees.reshape(nodes // block, block)
    sent1 = first_stage(
        slot_list, send_counts, degrees, w_neigh, grad_out, preact, features, neighbour_mean,
        tiles, last, scale,
    )
    got1 = exchange(sent1)
    grad_neighbour, st = node_stage(grad_out, preact, w_neigh, degrees)
    sent2 = terms(slot_list, send_counts, st, tiles, tuple(range(last)))

    extra = got1[:, block : block + EXTRA, :]
    share = jnp.sum(extra[:, :4, :].astype(F32), axis=0)
    share = share[:2] + share[2:]
    high = lax.reduce_precision(share, exponent_bits=8, mantissa_bits=7)
    low = share - high
    pay = jnp.concatenate([high, low, jnp.zeros((EXTRA - 4, width), F32)], axis=0).astype(BF16)
    sent2 = lax.dynamic_update_slice(
        sent2, jnp.broadcast_to(pay[None], (peers, EXTRA, width)), (0, last * block, 0)
    )
    got2 = exchange(sent2)
    cols = extra[:, 4, :8].astype(jnp.int32).T
    base = first_sum(cols, got1, grad_out, preact, w_self)
    grad_features, grad_w_self, grad_w_neigh = last_sum(cols, got2, base, last)
    return (grad_features.reshape(nodes, width), grad_neighbour, grad_w_self, grad_w_neigh)


def solution(mesh):
    placed = (
        P(AXES, None),
        P(AXES, None),
        P(AXES, None),
        P(AXES, None),
        P(),
        P(),
        P(AXES),
        P(AXES, None, None),
        P(AXES, None, None),
        P(AXES, None),
    )
    return jax.shard_map(
        body,
        mesh=mesh,
        in_specs=placed,
        out_specs=(P(AXES, None), P(AXES, None), P(), P()),
        check_vma=False,
    )
```

time: 223 us -> 203 us (0.910)
  Pallas kernels: 74 us -> 59.3 us
  waiting for transfers between devices: 125 us -> 122 us
    pallas_call x4, Pallas kernels: 52 us -> 37.3 us  [the longest x1 12.3 us: terms(): pl.pallas_call(functools.partial(term_kernel, slots, capacity, group), gr...]
    all_to_all x2, waiting for transfers between devices: 125 us -> 122 us  [exchange(): return lax.all_to_all(x, AXES, split_axis=0, concat_axis=0, tiled=True)]
  transfers between devices with their start and end apart: 2 -> 2, of which waited for: 2 -> 2; matrix products, arithmetic and copies ran while one was open for 1% -> 1% of each run, Pallas kernels for 17% -> 20%
where the time goes in v2:
time: 203 us; the launch traced here: 202 us
  waiting for transfers between devices  122 us (60%)
  Pallas kernels  59.3 us (29%)
  starting transfers between devices  17.2 us (8%)
    all_to_all x2, waiting for transfers between devices, exchange(): return lax.all_to_all(x, AXES, split_axis=0, concat_axis=0, tiled=True)  122 us
    pallas_call x1, Pallas kernels, first_sum(): pl.pallas_call(functools.partial(first_sum_kernel, group), grid_spec=pltp...  22 us
    all_to_all x2, starting transfers between devices, exchange(): return lax.all_to_all(x, AXES, split_axis=0, concat_axis=0, tiled=True)  17.2 us
    pallas_call x1, Pallas kernels, terms(): pl.pallas_call(functools.partial(term_kernel, slots, capacity, group), gr...  12.3 us
    pallas_call x1, Pallas kernels, last_sum(): pl.pallas_call(functools.partial(last_sum_kernel, slots, groups, parts),...  9.12 us
    pallas_call x1, Pallas kernels, first_stage(): pl.pallas_call(functools.partial(first_kernel, scale, slot, chunks, group...  8.8 us
    pallas_call x1, Pallas kernels, node_stage(): pl.pallas_call(node_kernel, grid=(rows // tile,), in_specs=[node, node, p...  7.07 us
  transfers between devices with their start and end apart: 2, of which 2 were waited for; matrix products, arithmetic and copies ran while one was open for 1% of the time, Pallas kernels for 20%

profile of v2, /device:TPU:7, one launch (start us, length us, event | category | flops | bytes accessed | tf_op | source)
XLA Modules:
  0.0 202.0 jit_solution(13235024079609544797)
XLA Ops:
  0.6 8.8 %first_stage.1 = bf16[128,136,128]{2,1,0:T(8,128)(2,1)} custom-call(s32[2,384]{1,0:T(2,128)} %bitcast.11, s32[1,128]{1,0:T(1,128)} %count_ref.1, s32[64,128]{1,0:T(8,128)} %bitcast.9, bf16[128,128]{1,0:T(8,128)(2,1)} %wn_ref.1, bf16[8192,128]{1,0:T(8,128)(2,1)} %grad_ref.3, bf16[8192,128]{1,0:T(8,128)(2,1)} %pre_ref.3, bf16[8192,128]{1,0:T(8,128)(2,1)} %feat_hbm.1, ...), custom_call_target="tpu_custom_call" | custom-call | flops 1342177280 | bytes 16777216 | tf_op jit(solution)/shard_map/first_stage/pallas_call | solution.py:235
  9.4 0.0 copy-start.1
  9.5 0.0 copy-start.2
  9.5 0.0 copy-start.5
  9.5 0.0 copy-start.6
  9.5 11.2 %all-to-all-start = ((bf16[128,136,128]{2,1,0:T(8,128)(2,1)}), bf16[128,136,128]{2,1,0:T(8,128)(2,1)}, u32[]{:S(2)}, u32[]{:S(2)}) async-start(bf16[128,136,128]{2,1,0:T(8,128)(2,1)} %first_stage.1), calls=%async_computation | async-start | bytes 8912896 | tf_op jit(solution)/shard_map/all_to_all | solution.py:403
  20.7 0.1 pad.2.clone
  20.8 0.0 copy-done.1
  20.8 0.0 copy-done.2
  20.8 7.1 %node_stage.1 = (bf16[8192,128]{1,0:T(8,128)(2,1)}, bf16[64,128,128]{2,1,0:T(8,128)(2,1)S(1)}) custom-call(bf16[8192,128]{1,0:T(8,128)(2,1)} %grad_ref.3, bf16[8192,128]{1,0:T(8,128)(2,1)} %pre_ref.3, bf16[128,128]{1,0:T(8,128)(2,1)S(1)} %copy-done.2, s32[64,128]{1,0:T(8,128)S(1)} %bitcast.10), custom_call_target="tpu_custom_call" | custom-call | flops 536870912 | bytes 8388608 | tf_op jit(solution)/shard_map/node_stage/pallas_call | solution.py:64
  27.9 0.0 copy-done.5
  27.9 0.0 copy-done.6
  27.9 12.3 %terms.1 = bf16[128,264,128]{2,1,0:T(8,128)(2,1)} custom-call(s32[2,384]{1,0:T(2,128)S(1)} %bitcast.12, s32[1,128]{1,0:T(1,128)S(1)} %copy-done.6, bf16[64,128,128]{2,1,0:T(8,128)(2,1)S(1)} %get-tuple-element.9.st_ref, bf16[128,3,128,128]{3,2,1,0:T(8,128)(2,1)} %bitcast.14), custom_call_target="tpu_custom_call" | custom-call | flops 1073741824 | bytes 16777216 | tf_op jit(solution)/shard_map/terms/pallas_call | solution.py:134
  40.2 34.4 %all-to-all-done.got_ref = bf16[128,136,128]{2,1,0:T(8,128)(2,1)} async-done(((bf16[128,136,128]{2,1,0:T(8,128)(2,1)}), bf16[128,136,128]{2,1,0:T(8,128)(2,1)}, u32[]{:S(2)}, u32[]{:S(2)}) %all-to-all-start) | async-done | bytes 4456480 | tf_op jit(solution)/shard_map/all_to_all | solution.py:403
  74.6 1.1 convert_reduce_fusion
  75.7 0.1 maximum_maximum_fusion
  75.7 0.8 broadcast_dynamic-update-slice_fusion
  76.5 0.0 copy-start
  76.5 0.0 copy-start.4
  76.5 6.0 %all-to-all-start.1 = ((bf16[128,264,128]{2,1,0:T(8,128)(2,1)}), bf16[128,264,128]{2,1,0:T(8,128)(2,1)}, u32[]{:S(2)}, u32[]{:S(2)}) async-start(bf16[128,264,128]{2,1,0:T(8,128)(2,1)} %broadcast_dynamic-update-slice_fusion), calls=%async_computation.1 | async-start | bytes 17301504 | tf_op jit(solution)/shard_map/all_to_all | solution.py:403
  82.5 1.0 slice.19
  83.5 0.1 copy.17
  83.6 0.0 copy-done
  83.6 0.0 copy-done.4
  83.6 0.0 copy-start.3
  83.6 22.0 %first_sum.1.base_hbm = f32[64,128,128]{2,1,0:T(8,128)} custom-call(s32[8,128]{1,0:T(8,128)S(1)} %convert_bitcast_fusion.cols_ref, bf16[128,136,128]{2,1,0:T(8,128)(2,1)} %all-to-all-done.got_ref, bf16[8192,128]{1,0:T(8,128)(2,1)S(1)} %copy-done, bf16[8192,128]{1,0:T(8,128)(2,1)} %pre_ref.3, bf16[128,128]{1,0:T(8,128)(2,1)S(1)} %copy-done.4), custom_call_target="tpu_custom_call" | custom-call | flops 268435456 | bytes 12845056 | tf_op jit(solution)/shard_map/first_sum/pallas_call | solution.py:292
  105.7 0.0 copy-done.3
  105.7 87.2 %all-to-all-done.1.got_hbm = bf16[128,264,128]{2,1,0:T(8,128)(2,1)} async-done(((bf16[128,264,128]{2,1,0:T(8,128)(2,1)}), bf16[128,264,128]{2,1,0:T(8,128)(2,1)}, u32[]{:S(2)}, u32[]{:S(2)}) %all-to-all-start.1) | async-done | bytes 8650784 | tf_op jit(solution)/shard_map/all_to_all | solution.py:403
  192.8 9.1 %last_sum.1 = (bf16[64,128,128]{2,1,0:T(8,128)(2,1)}, f32[128,128]{1,0:T(8,128)}, f32[128,128]{1,0:T(8,128)}) custom-call(s32[8,128]{1,0:T(8,128)} %copy-done.3, bf16[128,264,128]{2,1,0:T(8,128)(2,1)} %all-to-all-done.1.got_hbm, f32[64,128,128]{2,1,0:T(8,128)} %first_sum.1.base_hbm), custom_call_target="tpu_custom_call" | custom-call | flops 4325376 | bytes 14942208 | tf_op jit(solution)/shard_map/last_sum/pallas_call | solution.py:378
  (3 shorter events, 0.0 us)
Async XLA Ops:
  9.4 11.3 %copy-start.1 = (s32[8192]{0:T(1024)S(1)}, s32[8192]{0:T(1024)}, u32[]{:S(2)}) copy-start(s32[8192]{0:T(1024)} %param.16) | copy-start | bytes 98308
  9.5 11.3 %copy-start.2 = (bf16[128,128]{1,0:T(8,128)(2,1)S(1)}, bf16[128,128]{1,0:T(8,128)(2,1)}, u32[]{:S(2)}) copy-start(bf16[128,128]{1,0:T(8,128)(2,1)} %wn_ref.1) | copy-start | bytes 98308
  9.5 18.4 %copy-start.5 = (s32[1,2,384]{2,1,0:T(2,128)S(1)}, s32[1,2,384]{2,1,0:T(2,128)}, u32[]{:S(2)}) copy-start(s32[1,2,384]{2,1,0:T(2,128)} %param.18) | copy-start | bytes 9220
  9.5 18.4 %copy-start.6 = (s32[1,128]{1,0:T(1,128)S(1)}, s32[1,128]{1,0:T(1,128)}, u32[]{:S(2)}) copy-start(s32[1,128]{1,0:T(1,128)} %count_ref.1) | copy-start | bytes 1540
  9.5 65.1 %all-to-all-start = ((bf16[128,136,128]{2,1,0:T(8,128)(2,1)}), bf16[128,136,128]{2,1,0:T(8,128)(2,1)}, u32[]{:S(2)}, u32[]{:S(2)}) async-start(bf16[128,136,128]{2,1,0:T(8,128)(2,1)} %first_stage.1), calls=%async_computation | async-start | bytes 8912896 | tf_op jit(solution)/shard_map/all_to_all | solution.py:403
  76.5 7.1 %copy-start = (bf16[8192,128]{1,0:T(8,128)(2,1)S(1)}, bf16[8192,128]{1,0:T(8,128)(2,1)}, u32[]{:S(2)}) copy-start(bf16[8192,128]{1,0:T(8,128)(2,1)} %grad_ref.3) | copy-start | bytes 6291460
  76.5 7.1 %copy-start.4 = (bf16[128,128]{1,0:T(8,128)(2,1)S(1)}, bf16[128,128]{1,0:T(8,128)(2,1)}, u32[]{:S(2)}) copy-start(bf16[128,128]{1,0:T(8,128)(2,1)} %ws_ref.1) | copy-start | bytes 98308
  76.5 116.3 %all-to-all-start.1 = ((bf16[128,264,128]{2,1,0:T(8,128)(2,1)}), bf16[128,264,128]{2,1,0:T(8,128)(2,1)}, u32[]{:S(2)}, u32[]{:S(2)}) async-start(bf16[128,264,128]{2,1,0:T(8,128)(2,1)} %broadcast_dynamic-update-slice_fusion), calls=%async_computation.1 | async-start | bytes 17301504 | tf_op jit(solution)/shard_map/all_to_all | solution.py:403
  83.6 22.0 %copy-start.3 = (s32[8,128]{1,0:T(8,128)}, s32[8,128]{1,0:T(8,128)S(1)}, u32[]{:S(2)}) copy-start(s32[8,128]{1,0:T(8,128)S(1)} %convert_bitcast_fusion.cols_ref) | copy-start | bytes 12292

commit v3 on v2

--- a/solution.py
+++ b/solution.py
@@ -10,7 +10,8 @@
 
 BF16 = jnp.bfloat16
 F32 = jnp.float32
-AXES = ("gx", "gy")
+CORES = 2
+AXES = ("z", "core", "gy")
 NT = (((1,), (1,)), ((), ()))
 TN = (((0,), (0,)), ((), ()))
 VMEM_LIMIT = 50 * 1024 * 1024
@@ -34,6 +35,10 @@
 
 def local(index, blocks):
     return index & (blocks - 1) if blocks & (blocks - 1) == 0 else lax.rem(index, blocks)
+
+
+def order(group, cores):
+    return [d % (group // cores) * cores + d // (group // cores) for d in range(group)]
 
 
 def relu_of(grad_ref, pre_ref):
@@ -92,11 +97,11 @@
     return jnp.where(row < 4, out, jnp.where(row == 4, tail, 0.0))
 
 
-def term_rows(slots, capacity, group, step, list_ref, count_ref, st_ref, tile_ref, out_ref, at, transposed, share):
+def term_rows(slots, capacity, places, step, list_ref, count_ref, st_ref, tile_ref, out_ref, at, transposed, share):
     blocks, width, _ = st_ref.shape
     base = len(slots) * width
-    for d in range(group):
-        dest = step * group + d
+    for d, place in enumerate(places):
+        dest = step * len(places) + d
         for k, slot in enumerate(slots):
             rows_t = st_ref[local(list_ref[0, dest * capacity + slot], blocks)]
             if transposed:
@@ -104,7 +109,7 @@
             else:
                 term = dot(tile_ref[at + d, k], rows_t, (((0,), (1,)), ((), ())))
             keep = slot < count_ref[0, dest]
-            out_ref[at + d, k * width : (k + 1) * width, :] = jnp.where(keep, term, 0.0).astype(BF16)
+            out_ref[at + place, k * width : (k + 1) * width, :] = jnp.where(keep, term, 0.0).astype(BF16)
         if share is None:
             extra = jnp.zeros((EXTRA, width), BF16)
         else:
@@ -117,22 +122,23 @@
                 share[d : d + 1, width:],
                 jnp.broadcast_to(cols.astype(F32), (EXTRA, width)),
             ).astype(BF16)
-        out_ref[at + d, base : base + EXTRA, :] = extra
-
-
-def term_kernel(slots, capacity, group, list_ref, count_ref, st_ref, tile_ref, out_ref):
+        out_ref[at + place, base : base + EXTRA, :] = extra
+
+
+def term_kernel(slots, capacity, places, list_ref, count_ref, st_ref, tile_ref, out_ref):
     step = pl.program_id(0)
-    term_rows(slots, capacity, group, step, list_ref, count_ref, st_ref, tile_ref, out_ref, 0, False, None)
-
-
-def terms(tile_list, counts, st, tiles, slots, group=16):
+    term_rows(slots, capacity, places, step, list_ref, count_ref, st_ref, tile_ref, out_ref, 0, False, None)
+
+
+def terms(tile_list, counts, st, tiles, slots, places):
     peers, capacity, block, _ = tiles.shape
     blocks, width, _ = st.shape
     n = len(slots)
     at = slots[0] // n
+    group = len(places)
     rows = n * block + EXTRA
     return pl.pallas_call(
-        functools.partial(term_kernel, slots, capacity, group),
+        functools.partial(term_kernel, slots, capacity, places),
         grid_spec=pltpu.PrefetchScalarGridSpec(
             num_scalar_prefetch=2,
             grid=(peers // group,),
@@ -150,7 +156,7 @@
 
 
 def first_kernel(
-    scale, slot, chunks, groups,
+    scale, slot, chunks, places,
     list_hbm, count_hbm, deg_hbm, wn_hbm, grad_hbm, pre_hbm, feat_hbm, mean_hbm, tile_hbm,
     out_hbm,
     list_ref, count_ref, deg_ref, wn_ref, grad_ref, pre_ref, feat_ref, mean_ref, tile_ref, out_ref, st_ref, gw_ref,
@@ -159,7 +165,8 @@
     nodes, width = grad_ref.shape
     peers, capacity = tile_hbm.shape[:2]
     part = nodes // chunks
-    group = peers // groups
+    group = len(places)
+    groups = peers // group
     small = [
         pltpu.make_async_copy(src, dst, small_sem.at[i])
         for i, (src, dst) in enumerate(
@@ -216,7 +223,7 @@
         tile_copy(g).wait()
         share = gw_ref[pl.ds(pl.multiple_of(g * group, group), group), :]
         term_rows(
-            (slot,), capacity, group, g, list_ref, count_ref, st_ref,
+            (slot,), capacity, places, g, list_ref, count_ref, st_ref,
             tile_ref, out_ref, g * group, True, share,
         )
         out_copy(g).start()
@@ -225,15 +232,16 @@
         out_copy(g).wait()
 
 
-def first_stage(tile_list, counts, degrees, w_neigh, grad_out, preact, features, mean, tiles, slot, scale, chunks=4, groups=4):
+def first_stage(tile_list, counts, degrees, w_neigh, grad_out, preact, features, mean, tiles, slot, scale, places, chunks=2):
     nodes, width = grad_out.shape
     peers, capacity, block, _ = tiles.shape
     blocks = nodes // block
     rows = block + EXTRA
+    groups = peers // len(places)
     hbm = pl.BlockSpec(memory_space=pl.ANY)
     node = pltpu.VMEM((nodes, width), BF16)
     return pl.pallas_call(
-        functools.partial(first_kernel, scale, slot, chunks, groups),
+        functools.partial(first_kernel, scale, slot, chunks, places),
         in_specs=[hbm] * 9,
         out_specs=hbm,
         out_shape=jax.ShapeDtypeStruct((peers, rows, width), BF16),
@@ -311,12 +319,13 @@
 
 
 def last_sum_kernel(
-    slots, groups, parts, cols_ref, got_hbm, base_hbm, out_hbm, gs_ref, gn_ref,
+    slots, places, parts, cols_ref, got_hbm, base_hbm, out_hbm, gs_ref, gn_ref,
     got, out, acc, gw, got_sem, base_sem, out_sem,
 ):
     peers = got.shape[0]
     blocks, block, width = acc.shape[1:]
-    group = peers // groups
+    group = len(places)
+    groups = peers // group
     part = blocks // parts
 
     def got_copy(g):
@@ -342,18 +351,18 @@
     @pl.loop(0, groups)
     def _(g):
         got_copy(g).wait()
-        for d8 in range(0, group, 8):
-            shares = []
-            for d in range(d8, d8 + 8):
-                src = g * group + d
-                for k in range(slots):
-                    col = cols_ref[k, src]
-                    acc[k, col] += got[src, k * block : (k + 1) * block, :].astype(F32)
-                extra = got[src, slots * block : slots * block + EXTRA, :].astype(F32)
-                shares.append(extra[:2] + extra[2:4])
-            at = pl.ds(pl.multiple_of(g * group + d8, 8), 8)
-            gw[at, :width] = jnp.concatenate([share[:1] for share in shares], axis=0)
-            gw[at, width:] = jnp.concatenate([share[1:] for share in shares], axis=0)
+        shares = []
+        for d in range(group):
+            src = g * group + d
+            for k in range(slots):
+                col = cols_ref[k, src]
+                acc[k, col] += got[src, k * block : (k + 1) * block, :].astype(F32)
+            extra = got[src, slots * block : slots * block + EXTRA, :].astype(F32)
+            shares.append(extra[:2] + extra[2:4])
+        shares = [shares[place] for place in places]
+        at = pl.ds(pl.multiple_of(g * group, group), group)
+        gw[at, :width] = jnp.concatenate([share[:1] for share in shares], axis=0)
+        gw[at, width:] = jnp.concatenate([share[1:] for share in shares], axis=0)
 
     @pl.loop(0, parts)
     def _(p):
@@ -370,13 +379,14 @@
         out_copy(p).wait()
 
 
-def last_sum(cols, got, base, slots, groups=4, parts=4):
+def last_sum(cols, got, base, slots, places, parts=4):
     peers, rows, width = got.shape
     blocks, block, _ = base.shape
+    groups = peers // len(places)
     hbm = pl.BlockSpec(memory_space=pl.ANY)
     vmem = pl.BlockSpec(memory_space=pltpu.VMEM)
     return pl.pallas_call(
-        functools.partial(last_sum_kernel, slots, groups, parts),
+        functools.partial(last_sum_kernel, slots, places, parts),
         in_specs=[pl.BlockSpec(memory_space=pltpu.SMEM), hbm, hbm],
         out_specs=[hbm, vmem, vmem],
         scratch_shapes=[
@@ -400,7 +410,7 @@
 
 
 def exchange(x):
-    return lax.all_to_all(x, AXES, split_axis=0, concat_axis=0, tiled=True)
+    return lax.all_to_all(x, ("z", "gy", "core"), split_axis=0, concat_axis=0, tiled=True)
 
 
 def body(
@@ -417,7 +427,10 @@
 ):
     nodes, width = grad_out.shape
     block = tile_values.shape[1]
-    peers = lax.axis_size("gx") * lax.axis_size("gy")
+    cores = lax.axis_size("core")
+    group = cores * lax.axis_size("gy")
+    peers = lax.axis_size("z") * group
+    places = order(group, cores)
     capacity = tile_values.shape[0] // peers
     scale = 1.0 / math.sqrt(nodes * peers)
     slot_list = tile_list[0]
@@ -427,11 +440,11 @@
     degrees = degrees.reshape(nodes // block, block)
     sent1 = first_stage(
         slot_list, send_counts, degrees, w_neigh, grad_out, preact, features, neighbour_mean,
-        tiles, last, scale,
+        tiles, last, scale, places,
     )
     got1 = exchange(sent1)
     grad_neighbour, st = node_stage(grad_out, preact, w_neigh, degrees)
-    sent2 = terms(slot_list, send_counts, st, tiles, tuple(range(last)))
+    sent2 = terms(slot_list, send_counts, st, tiles, tuple(range(last)), places)
 
     extra = got1[:, block : block + EXTRA, :]
     share = jnp.sum(extra[:, :4, :].astype(F32), axis=0)
@@ -445,11 +458,13 @@
     got2 = exchange(sent2)
     cols = extra[:, 4, :8].astype(jnp.int32).T
     base = first_sum(cols, got1, grad_out, preact, w_self)
-    grad_features, grad_w_self, grad_w_neigh = last_sum(cols, got2, base, last)
+    grad_features, grad_w_self, grad_w_neigh = last_sum(cols, got2, base, last, places)
     return (grad_features.reshape(nodes, width), grad_neighbour, grad_w_self, grad_w_neigh)
 
 
 def solution(mesh):
+    major, minor = mesh.devices.shape
+    mesh = jax.sharding.Mesh(mesh.devices.reshape(major // CORES, CORES, minor), AXES)
     placed = (
         P(AXES, None),
         P(AXES, None),

time: 203 us -> 197 us (0.970)
  waiting for transfers between devices: 122 us -> 115 us
    all_to_all x2, waiting for transfers between devices: 122 us -> 115 us  [exchange(): lax.all_to_all(x, ('z', 'gy', 'core'), split_axis=0, concat_axis=0, tiled...]
where the time goes in v3:
time: 197 us; the launch traced here: 195 us
  waiting for transfers between devices  115 us (58%)
  Pallas kernels  57.8 us (29%)
  starting transfers between devices  18.8 us (10%)
  local copies, waits for them, and re-layouts  1.97 us (1%)
    all_to_all x2, waiting for transfers between devices, exchange(): lax.all_to_all(x, ('z', 'gy', 'core'), split_axis=0, concat_axis=0, tiled...  115 us
    pallas_call x1, Pallas kernels, first_sum(): pl.pallas_call(functools.partial(first_sum_kernel, group), grid_spec=pltp...  22 us
    all_to_all x2, starting transfers between devices, exchange(): lax.all_to_all(x, ('z', 'gy', 'core'), split_axis=0, concat_axis=0, tiled...  18.8 us
    pallas_call x1, Pallas kernels, terms(): pl.pallas_call(functools.partial(term_kernel, slots, capacity, places), g...  10.9 us
    pallas_call x1, Pallas kernels, last_sum(): pl.pallas_call(functools.partial(last_sum_kernel, slots, places, parts),...  9.36 us
    pallas_call x1, Pallas kernels, first_stage(): pl.pallas_call(functools.partial(first_kernel, scale, slot, chunks, place...  8.45 us
    pallas_call x1, Pallas kernels, node_stage(): pl.pallas_call(node_kernel, grid=(rows // tile,), in_specs=[node, node, p...  7.06 us
  transfers between devices with their start and end apart: 2, of which 2 were waited for; matrix products, arithmetic and copies ran while one was open for 1% of the time, Pallas kernels for 20%

profile of v3, /device:TPU:7, one launch (start us, length us, event | category | flops | bytes accessed | tf_op | source)
XLA Modules:
  0.0 195.5 jit_solution(17197426997483190882)
XLA Ops:
  0.6 8.4 %first_stage.1 = bf16[128,136,128]{2,1,0:T(8,128)(2,1)} custom-call(s32[2,384]{1,0:T(2,128)} %bitcast.11, s32[1,128]{1,0:T(1,128)} %count_ref.1, s32[64,128]{1,0:T(8,128)} %bitcast.9, bf16[128,128]{1,0:T(8,128)(2,1)} %wn_ref.1, bf16[8192,128]{1,0:T(8,128)(2,1)} %grad_ref.3, bf16[8192,128]{1,0:T(8,128)(2,1)} %pre_ref.3, bf16[8192,128]{1,0:T(8,128)(2,1)} %feat_hbm.1, ...), custom_call_target="tpu_custom_call" | custom-call | flops 1342177280 | bytes 16777216 | tf_op jit(solution)/shard_map/first_stage/pallas_call | solution.py:243
  9.1 0.0 copy-start.1
  9.1 0.0 copy-start.2
  9.1 0.0 copy-start.5
  9.1 0.0 copy-start.6
  9.1 11.2 %all-to-all-start = ((bf16[128,136,128]{2,1,0:T(8,128)(2,1)}), bf16[128,136,128]{2,1,0:T(8,128)(2,1)}, u32[]{:S(2)}, u32[]{:S(2)}) async-start(bf16[128,136,128]{2,1,0:T(8,128)(2,1)} %first_stage.1), calls=%async_computation | async-start | bytes 8912896 | tf_op jit(solution)/shard_map/all_to_all | solution.py:413
  20.3 0.1 pad.2.clone
  20.4 0.0 copy-done.1
  20.4 0.0 copy-done.2
  20.4 7.1 %node_stage.1 = (bf16[8192,128]{1,0:T(8,128)(2,1)}, bf16[64,128,128]{2,1,0:T(8,128)(2,1)S(1)}) custom-call(bf16[8192,128]{1,0:T(8,128)(2,1)} %grad_ref.3, bf16[8192,128]{1,0:T(8,128)(2,1)} %pre_ref.3, bf16[128,128]{1,0:T(8,128)(2,1)S(1)} %copy-done.2, s32[64,128]{1,0:T(8,128)S(1)} %bitcast.10), custom_call_target="tpu_custom_call" | custom-call | flops 536870912 | bytes 8388608 | tf_op jit(solution)/shard_map/node_stage/pallas_call | solution.py:69
  27.5 0.0 copy-done.5
  27.5 0.0 copy-done.6
  27.5 10.9 %terms.1 = bf16[128,264,128]{2,1,0:T(8,128)(2,1)} custom-call(s32[2,384]{1,0:T(2,128)S(1)} %bitcast.12, s32[1,128]{1,0:T(1,128)S(1)} %copy-done.6, bf16[64,128,128]{2,1,0:T(8,128)(2,1)S(1)} %get-tuple-element.9.st_ref, bf16[128,3,128,128]{3,2,1,0:T(8,128)(2,1)} %bitcast.14), custom_call_target="tpu_custom_call" | custom-call | flops 1073741824 | bytes 16777216 | tf_op jit(solution)/shard_map/terms/pallas_call | solution.py:140
  38.4 35.6 %all-to-all-done.got_ref = bf16[128,136,128]{2,1,0:T(8,128)(2,1)} async-done(((bf16[128,136,128]{2,1,0:T(8,128)(2,1)}), bf16[128,136,128]{2,1,0:T(8,128)(2,1)}, u32[]{:S(2)}, u32[]{:S(2)}) %all-to-all-start) | async-done | bytes 4456480 | tf_op jit(solution)/shard_map/all_to_all | solution.py:413
  74.0 1.1 convert_reduce_fusion
  75.1 0.1 maximum_maximum_fusion
  75.2 0.8 broadcast_dynamic-update-slice_fusion
  76.0 0.0 copy-start
  76.0 0.0 copy-start.4
  76.0 7.6 %all-to-all-start.1 = ((bf16[128,264,128]{2,1,0:T(8,128)(2,1)}), bf16[128,264,128]{2,1,0:T(8,128)(2,1)}, u32[]{:S(2)}, u32[]{:S(2)}) async-start(bf16[128,264,128]{2,1,0:T(8,128)(2,1)} %broadcast_dynamic-update-slice_fusion), calls=%async_computation.1 | async-start | bytes 17301504 | tf_op jit(solution)/shard_map/all_to_all | solution.py:413
  83.6 1.0 slice.19
  84.6 0.1 copy.17
  84.7 0.0 copy-done
  84.7 0.0 copy-done.4
  84.7 0.0 copy-start.3
  84.7 22.0 %first_sum.1.base_hbm = f32[64,128,128]{2,1,0:T(8,128)} custom-call(s32[8,128]{1,0:T(8,128)S(1)} %convert_bitcast_fusion.cols_ref, bf16[128,136,128]{2,1,0:T(8,128)(2,1)} %all-to-all-done.got_ref, bf16[8192,128]{1,0:T(8,128)(2,1)S(1)} %copy-done, bf16[8192,128]{1,0:T(8,128)(2,1)} %pre_ref.3, bf16[128,128]{1,0:T(8,128)(2,1)S(1)} %copy-done.4), custom_call_target="tpu_custom_call" | custom-call | flops 268435456 | bytes 12845056 | tf_op jit(solution)/shard_map/first_sum/pallas_call | solution.py:300
  106.8 0.0 copy-done.3
  106.8 79.4 %all-to-all-done.1.got_hbm = bf16[128,264,128]{2,1,0:T(8,128)(2,1)} async-done(((bf16[128,264,128]{2,1,0:T(8,128)(2,1)}), bf16[128,264,128]{2,1,0:T(8,128)(2,1)}, u32[]{:S(2)}, u32[]{:S(2)}) %all-to-all-start.1) | async-done | bytes 8650784 | tf_op jit(solution)/shard_map/all_to_all | solution.py:413
  186.1 9.4 %last_sum.1 = (bf16[64,128,128]{2,1,0:T(8,128)(2,1)}, f32[128,128]{1,0:T(8,128)}, f32[128,128]{1,0:T(8,128)}) custom-call(s32[8,128]{1,0:T(8,128)} %copy-done.3, bf16[128,264,128]{2,1,0:T(8,128)(2,1)} %all-to-all-done.1.got_hbm, f32[64,128,128]{2,1,0:T(8,128)} %first_sum.1.base_hbm), custom_call_target="tpu_custom_call" | custom-call | flops 4325376 | bytes 14942208 | tf_op jit(solution)/shard_map/last_sum/pallas_call | solution.py:388
  (3 shorter events, 0.0 us)
Async XLA Ops:
  9.1 11.3 %copy-start.1 = (s32[8192]{0:T(1024)S(1)}, s32[8192]{0:T(1024)}, u32[]{:S(2)}) copy-start(s32[8192]{0:T(1024)} %param.16) | copy-start | bytes 98308
  9.1 11.3 %copy-start.2 = (bf16[128,128]{1,0:T(8,128)(2,1)S(1)}, bf16[128,128]{1,0:T(8,128)(2,1)}, u32[]{:S(2)}) copy-start(bf16[128,128]{1,0:T(8,128)(2,1)} %wn_ref.1) | copy-start | bytes 98308
  9.1 18.4 %copy-start.5 = (s32[1,2,384]{2,1,0:T(2,128)S(1)}, s32[1,2,384]{2,1,0:T(2,128)}, u32[]{:S(2)}) copy-start(s32[1,2,384]{2,1,0:T(2,128)} %param.18) | copy-start | bytes 9220
  9.1 18.4 %copy-start.6 = (s32[1,128]{1,0:T(1,128)S(1)}, s32[1,128]{1,0:T(1,128)}, u32[]{:S(2)}) copy-start(s32[1,128]{1,0:T(1,128)} %count_ref.1) | copy-start | bytes 1540
  9.1 64.9 %all-to-all-start = ((bf16[128,136,128]{2,1,0:T(8,128)(2,1)}), bf16[128,136,128]{2,1,0:T(8,128)(2,1)}, u32[]{:S(2)}, u32[]{:S(2)}) async-start(bf16[128,136,128]{2,1,0:T(8,128)(2,1)} %first_stage.1), calls=%async_computation | async-start | bytes 8912896 | tf_op jit(solution)/shard_map/all_to_all | solution.py:413
  76.0 8.8 %copy-start = (bf16[8192,128]{1,0:T(8,128)(2,1)S(1)}, bf16[8192,128]{1,0:T(8,128)(2,1)}, u32[]{:S(2)}) copy-start(bf16[8192,128]{1,0:T(8,128)(2,1)} %grad_ref.3) | copy-start | bytes 6291460
  76.0 8.8 %copy-start.4 = (bf16[128,128]{1,0:T(8,128)(2,1)S(1)}, bf16[128,128]{1,0:T(8,128)(2,1)}, u32[]{:S(2)}) copy-start(bf16[128,128]{1,0:T(8,128)(2,1)} %ws_ref.1) | copy-start | bytes 98308
  76.0 110.2 %all-to-all-start.1 = ((bf16[128,264,128]{2,1,0:T(8,128)(2,1)}), bf16[128,264,128]{2,1,0:T(8,128)(2,1)}, u32[]{:S(2)}, u32[]{:S(2)}) async-start(bf16[128,264,128]{2,1,0:T(8,128)(2,1)} %broadcast_dynamic-update-slice_fusion), calls=%async_computation.1 | async-start | bytes 17301504 | tf_op jit(solution)/shard_map/all_to_all | solution.py:413
  84.7 22.0 %copy-start.3 = (s32[8,128]{1,0:T(8,128)}, s32[8,128]{1,0:T(8,128)S(1)}, u32[]{:S(2)}) copy-start(s32[8,128]{1,0:T(8,128)S(1)} %convert_bitcast_fusion.cols_ref) | copy-start | bytes 12292

commit v4 on v3

--- a/solution.py
+++ b/solution.py
@@ -320,10 +320,10 @@
 
 def last_sum_kernel(
     slots, places, parts, cols_ref, got_hbm, base_hbm, out_hbm, gs_ref, gn_ref,
-    got, out, acc, gw, got_sem, base_sem, out_sem,
+    got, out, base, acc, gw, got_sem, base_sem, out_sem,
 ):
     peers = got.shape[0]
-    blocks, block, width = acc.shape[1:]
+    blocks, block, width = acc.shape
     group = len(places)
     groups = peers // group
     part = blocks // parts
@@ -336,17 +336,14 @@
         at = pl.ds(p * part, part)
         return pltpu.make_async_copy(out.at[at], out_hbm.at[at], out_sem.at[p])
 
-    load = pltpu.make_async_copy(base_hbm, acc.at[0], base_sem)
-    load.start()
+    load = pltpu.make_async_copy(base_hbm, base, base_sem)
     for g in range(groups):
         got_copy(g).start()
-
-    for k in range(1, slots):
-        @pl.loop(0, blocks, unroll=4)
-        def _(b):
-            acc[k, b] = jnp.zeros((block, width), F32)
-
-    load.wait()
+    load.start()
+
+    @pl.loop(0, blocks, unroll=4)
+    def _(b):
+        acc[b] = jnp.zeros((block, width), F32)
 
     @pl.loop(0, groups)
     def _(g):
@@ -356,7 +353,7 @@
             src = g * group + d
             for k in range(slots):
                 col = cols_ref[k, src]
-                acc[k, col] += got[src, k * block : (k + 1) * block, :].astype(F32)
+                acc[col] += got[src, k * block : (k + 1) * block, :].astype(F32)
             extra = got[src, slots * block : slots * block + EXTRA, :].astype(F32)
             shares.append(extra[:2] + extra[2:4])
         shares = [shares[place] for place in places]
@@ -364,13 +361,13 @@
         gw[at, :width] = jnp.concatenate([share[:1] for share in shares], axis=0)
         gw[at, width:] = jnp.concatenate([share[1:] for share in shares], axis=0)
 
+    load.wait()
+
     @pl.loop(0, parts)
     def _(p):
         for b in range(part):
-            total = acc[0, p * part + b]
-            for k in range(1, slots):
-                total += acc[k, p * part + b]
-            out[p * part + b] = total.astype(BF16)
+            at = p * part + b
+            out[at] = (base[at] + acc[at]).astype(BF16)
         out_copy(p).start()
 
     gs_ref[...] = gw[:, :width].T
@@ -392,7 +389,8 @@
         scratch_shapes=[
             pltpu.VMEM((peers, rows, width), BF16),
             pltpu.VMEM((blocks, block, width), BF16),
-            pltpu.VMEM((slots, blocks, block, width), F32),
+            pltpu.VMEM((blocks, block, width), F32),
+            pltpu.VMEM((blocks, block, width), F32),
             pltpu.VMEM((width, 2 * width), F32),
             pltpu.SemaphoreType.DMA((groups,)),
             pltpu.SemaphoreType.DMA,

time: 197 us -> 195 us (0.990)
  transfers between devices with their start and end apart: 2 -> 2, of which waited for: 2 -> 2; matrix products, arithmetic and copies ran while one was open for 1% -> 1% of each run, Pallas kernels for 20% -> 21%
where the time goes in v4:
time: 195 us; the launch traced here: 194 us
  waiting for transfers between devices  115 us (59%)
  Pallas kernels  56 us (29%)
  starting transfers between devices  18.8 us (10%)
  local copies, waits for them, and re-layouts  1.97 us (1%)
    all_to_all x2, waiting for transfers between devices, exchange(): lax.all_to_all(x, ('z', 'gy', 'core'), split_axis=0, concat_axis=0, tiled...  115 us
    pallas_call x1, Pallas kernels, first_sum(): pl.pallas_call(functools.partial(first_sum_kernel, group), grid_spec=pltp...  22 us
    all_to_all x2, starting transfers between devices, exchange(): lax.all_to_all(x, ('z', 'gy', 'core'), split_axis=0, concat_axis=0, tiled...  18.8 us
    pallas_call x1, Pallas kernels, terms(): pl.pallas_call(functools.partial(term_kernel, slots, capacity, places), g...  10.9 us
    pallas_call x1, Pallas kernels, first_stage(): pl.pallas_call(functools.partial(first_kernel, scale, slot, chunks, place...  8.45 us
    pallas_call x1, Pallas kernels, last_sum(): pl.pallas_call(functools.partial(last_sum_kernel, slots, places, parts),...  7.59 us
    pallas_call x1, Pallas kernels, node_stage(): pl.pallas_call(node_kernel, grid=(rows // tile,), in_specs=[node, node, p...  7.06 us
  transfers between devices with their start and end apart: 2, of which 2 were waited for; matrix products, arithmetic and copies ran while one was open for 1% of the time, Pallas kernels for 21%

profile of v4, /device:TPU:7, one launch (start us, length us, event | category | flops | bytes accessed | tf_op | source)
XLA Modules:
  0.0 193.7 jit_solution(5569338433622157656)
XLA Ops:
  0.6 8.4 %first_stage.1 = bf16[128,136,128]{2,1,0:T(8,128)(2,1)} custom-call(s32[2,384]{1,0:T(2,128)} %bitcast.11, s32[1,128]{1,0:T(1,128)} %count_ref.1, s32[64,128]{1,0:T(8,128)} %bitcast.9, bf16[128,128]{1,0:T(8,128)(2,1)} %wn_ref.1, bf16[8192,128]{1,0:T(8,128)(2,1)} %grad_ref.3, bf16[8192,128]{1,0:T(8,128)(2,1)} %pre_ref.3, bf16[8192,128]{1,0:T(8,128)(2,1)} %feat_hbm.1, ...), custom_call_target="tpu_custom_call" | custom-call | flops 1342177280 | bytes 16777216 | tf_op jit(solution)/shard_map/first_stage/pallas_call | solution.py:243
  9.1 0.0 copy-start.1
  9.1 0.0 copy-start.2
  9.1 0.0 copy-start.5
  9.1 0.0 copy-start.6
  9.1 11.2 %all-to-all-start = ((bf16[128,136,128]{2,1,0:T(8,128)(2,1)}), bf16[128,136,128]{2,1,0:T(8,128)(2,1)}, u32[]{:S(2)}, u32[]{:S(2)}) async-start(bf16[128,136,128]{2,1,0:T(8,128)(2,1)} %first_stage.1), calls=%async_computation | async-start | bytes 8912896 | tf_op jit(solution)/shard_map/all_to_all | solution.py:411
  20.3 0.1 pad.2.clone
  20.4 0.0 copy-done.1
  20.4 0.0 copy-done.2
  20.4 7.1 %node_stage.1 = (bf16[8192,128]{1,0:T(8,128)(2,1)}, bf16[64,128,128]{2,1,0:T(8,128)(2,1)S(1)}) custom-call(bf16[8192,128]{1,0:T(8,128)(2,1)} %grad_ref.3, bf16[8192,128]{1,0:T(8,128)(2,1)} %pre_ref.3, bf16[128,128]{1,0:T(8,128)(2,1)S(1)} %copy-done.2, s32[64,128]{1,0:T(8,128)S(1)} %bitcast.10), custom_call_target="tpu_custom_call" | custom-call | flops 536870912 | bytes 8388608 | tf_op jit(solution)/shard_map/node_stage/pallas_call | solution.py:69
  27.5 0.0 copy-done.5
  27.5 0.0 copy-done.6
  27.5 10.9 %terms.1 = bf16[128,264,128]{2,1,0:T(8,128)(2,1)} custom-call(s32[2,384]{1,0:T(2,128)S(1)} %bitcast.12, s32[1,128]{1,0:T(1,128)S(1)} %copy-done.6, bf16[64,128,128]{2,1,0:T(8,128)(2,1)S(1)} %get-tuple-element.9.st_ref, bf16[128,3,128,128]{3,2,1,0:T(8,128)(2,1)} %bitcast.14), custom_call_target="tpu_custom_call" | custom-call | flops 1073741824 | bytes 16777216 | tf_op jit(solution)/shard_map/terms/pallas_call | solution.py:140
  38.4 35.6 %all-to-all-done.got_ref = bf16[128,136,128]{2,1,0:T(8,128)(2,1)} async-done(((bf16[128,136,128]{2,1,0:T(8,128)(2,1)}), bf16[128,136,128]{2,1,0:T(8,128)(2,1)}, u32[]{:S(2)}, u32[]{:S(2)}) %all-to-all-start) | async-done | bytes 4456480 | tf_op jit(solution)/shard_map/all_to_all | solution.py:411
  74.0 1.1 convert_reduce_fusion
  75.1 0.1 maximum_maximum_fusion
  75.2 0.8 broadcast_dynamic-update-slice_fusion
  76.0 0.0 copy-start
  76.0 0.0 copy-start.4
  76.0 7.6 %all-to-all-start.1 = ((bf16[128,264,128]{2,1,0:T(8,128)(2,1)}), bf16[128,264,128]{2,1,0:T(8,128)(2,1)}, u32[]{:S(2)}, u32[]{:S(2)}) async-start(bf16[128,264,128]{2,1,0:T(8,128)(2,1)} %broadcast_dynamic-update-slice_fusion), calls=%async_computation.1 | async-start | bytes 17301504 | tf_op jit(solution)/shard_map/all_to_all | solution.py:411
  83.6 1.0 slice.19
  84.6 0.1 copy.17
  84.7 0.0 copy-done
  84.7 0.0 copy-done.4
  84.7 0.0 copy-start.3
  84.7 22.0 %first_sum.1.base_hbm = f32[64,128,128]{2,1,0:T(8,128)} custom-call(s32[8,128]{1,0:T(8,128)S(1)} %convert_bitcast_fusion.cols_ref, bf16[128,136,128]{2,1,0:T(8,128)(2,1)} %all-to-all-done.got_ref, bf16[8192,128]{1,0:T(8,128)(2,1)S(1)} %copy-done, bf16[8192,128]{1,0:T(8,128)(2,1)} %pre_ref.3, bf16[128,128]{1,0:T(8,128)(2,1)S(1)} %copy-done.4), custom_call_target="tpu_custom_call" | custom-call | flops 268435456 | bytes 12845056 | tf_op jit(solution)/shard_map/first_sum/pallas_call | solution.py:300
  106.8 0.0 copy-done.3
  106.8 79.4 %all-to-all-done.1.got_hbm = bf16[128,264,128]{2,1,0:T(8,128)(2,1)} async-done(((bf16[128,264,128]{2,1,0:T(8,128)(2,1)}), bf16[128,264,128]{2,1,0:T(8,128)(2,1)}, u32[]{:S(2)}, u32[]{:S(2)}) %all-to-all-start.1) | async-done | bytes 8650784 | tf_op jit(solution)/shard_map/all_to_all | solution.py:411
  186.1 7.6 %last_sum.1 = (bf16[64,128,128]{2,1,0:T(8,128)(2,1)}, f32[128,128]{1,0:T(8,128)}, f32[128,128]{1,0:T(8,128)}) custom-call(s32[8,128]{1,0:T(8,128)} %copy-done.3, bf16[128,264,128]{2,1,0:T(8,128)(2,1)} %all-to-all-done.1.got_hbm, f32[64,128,128]{2,1,0:T(8,128)} %first_sum.1.base_hbm), custom_call_target="tpu_custom_call" | custom-call | flops 4325376 | bytes 14942208 | tf_op jit(solution)/shard_map/last_sum/pallas_call | solution.py:385
  (3 shorter events, 0.0 us)
Async XLA Ops:
  9.1 11.3 %copy-start.1 = (s32[8192]{0:T(1024)S(1)}, s32[8192]{0:T(1024)}, u32[]{:S(2)}) copy-start(s32[8192]{0:T(1024)} %param.16) | copy-start | bytes 98308
  9.1 11.3 %copy-start.2 = (bf16[128,128]{1,0:T(8,128)(2,1)S(1)}, bf16[128,128]{1,0:T(8,128)(2,1)}, u32[]{:S(2)}) copy-start(bf16[128,128]{1,0:T(8,128)(2,1)} %wn_ref.1) | copy-start | bytes 98308
  9.1 18.4 %copy-start.5 = (s32[1,2,384]{2,1,0:T(2,128)S(1)}, s32[1,2,384]{2,1,0:T(2,128)}, u32[]{:S(2)}) copy-start(s32[1,2,384]{2,1,0:T(2,128)} %param.18) | copy-start | bytes 9220
  9.1 18.4 %copy-start.6 = (s32[1,128]{1,0:T(1,128)S(1)}, s32[1,128]{1,0:T(1,128)}, u32[]{:S(2)}) copy-start(s32[1,128]{1,0:T(1,128)} %count_ref.1) | copy-start | bytes 1540
  9.1 64.9 %all-to-all-start = ((bf16[128,136,128]{2,1,0:T(8,128)(2,1)}), bf16[128,136,128]{2,1,0:T(8,128)(2,1)}, u32[]{:S(2)}, u32[]{:S(2)}) async-start(bf16[128,136,128]{2,1,0:T(8,128)(2,1)} %first_stage.1), calls=%async_computation | async-start | bytes 8912896 | tf_op jit(solution)/shard_map/all_to_all | solution.py:411
  76.0 8.8 %copy-start = (bf16[8192,128]{1,0:T(8,128)(2,1)S(1)}, bf16[8192,128]{1,0:T(8,128)(2,1)}, u32[]{:S(2)}) copy-start(bf16[8192,128]{1,0:T(8,128)(2,1)} %grad_ref.3) | copy-start | bytes 6291460
  76.0 8.8 %copy-start.4 = (bf16[128,128]{1,0:T(8,128)(2,1)S(1)}, bf16[128,128]{1,0:T(8,128)(2,1)}, u32[]{:S(2)}) copy-start(bf16[128,128]{1,0:T(8,128)(2,1)} %ws_ref.1) | copy-start | bytes 98308
  76.0 110.2 %all-to-all-start.1 = ((bf16[128,264,128]{2,1,0:T(8,128)(2,1)}), bf16[128,264,128]{2,1,0:T(8,128)(2,1)}, u32[]{:S(2)}, u32[]{:S(2)}) async-start(bf16[128,264,128]{2,1,0:T(8,128)(2,1)} %broadcast_dynamic-update-slice_fusion), calls=%async_computation.1 | async-start | bytes 17301504 | tf_op jit(solution)/shard_map/all_to_all | solution.py:411
  84.7 22.0 %copy-start.3 = (s32[8,128]{1,0:T(8,128)}, s32[8,128]{1,0:T(8,128)S(1)}, u32[]{:S(2)}) copy-start(s32[8,128]{1,0:T(8,128)S(1)} %convert_bitcast_fusion.cols_ref) | copy-start | bytes 12292

commit v5 on v4

--- a/solution.py
+++ b/solution.py
@@ -159,7 +159,7 @@
     scale, slot, chunks, places,
     list_hbm, count_hbm, deg_hbm, wn_hbm, grad_hbm, pre_hbm, feat_hbm, mean_hbm, tile_hbm,
     out_hbm,
-    list_ref, count_ref, deg_ref, wn_ref, grad_ref, pre_ref, feat_ref, mean_ref, tile_ref, out_ref, st_ref, gw_ref,
+    list_ref, count_ref, deg_ref, wn_ref, grad_ref, pre_ref, feat_ref, mean_ref, tile_ref, out_ref, st_ref, gw_ref, relu_ref,
     small_sem, node_sem, tile_sem, out_sem,
 ):
     nodes, width = grad_ref.shape
@@ -192,9 +192,10 @@
 
     for copy in small[:2]:
         copy.start()
-    for c in range(chunks):
-        for copy in node_copies(c):
-            copy.start()
+    for half in (slice(0, 2), slice(2, 4)):
+        for c in range(chunks):
+            for copy in node_copies(c)[half]:
+                copy.start()
     for copy in small[2:]:
         copy.start()
     for g in range(groups):
@@ -205,13 +206,21 @@
 
     @pl.loop(0, chunks)
     def _(c):
-        for copy in node_copies(c):
+        for copy in node_copies(c)[:2]:
             copy.wait()
         at = pl.ds(pl.multiple_of(c * part, part), part)
         relu_t = relu_of(grad_ref.at[at], pre_ref.at[at]).T
+        relu_ref[c] = relu_t
         rows = part // deg_ref.shape[1]
         deg = deg_ref[pl.ds(pl.multiple_of(c * rows, rows), rows), :]
         scaled_rows(wn_ref[...], relu_t, deg, st_ref, c * rows)
+
+    @pl.loop(0, chunks)
+    def _(c):
+        for copy in node_copies(c)[2:]:
+            copy.wait()
+        at = pl.ds(pl.multiple_of(c * part, part), part)
+        relu_t = relu_ref[c]
         gw_ref[:, :width] += dot(relu_t, feat_ref[at, :]) * scale
         gw_ref[:, width:] += dot(relu_t, mean_ref[at, :]) * scale
 
@@ -258,6 +267,7 @@
             pltpu.VMEM((peers, rows, width), BF16),
             pltpu.VMEM((blocks, width, block), BF16),
             pltpu.VMEM((width, 2 * width), F32),
+            pltpu.VMEM((chunks, width, nodes // chunks), BF16),
             pltpu.SemaphoreType.DMA((4,)),
             pltpu.SemaphoreType.DMA((4, chunks)),
             pltpu.SemaphoreType.DMA((groups,)),
@@ -438,7 +448,7 @@
     degrees = degrees.reshape(nodes // block, block)
     sent1 = first_stage(
         slot_list, send_counts, degrees, w_neigh, grad_out, preact, features, neighbour_mean,
-        tiles, last, scale, places,
+        tiles, last, scale, places + [group + place for place in places],
     )
     got1 = exchange(sent1)
     grad_neighbour, st = node_stage(grad_out, preact, w_neigh, degrees)

time: 195 us -> 194 us (level)
  no operation moved by 1% of the time
where the time goes in v5:
time: 194 us; the launch traced here: 193 us
  waiting for transfers between devices  115 us (59%)
  Pallas kernels  55.5 us (29%)
  starting transfers between devices  18.8 us (10%)
  local copies, waits for them, and re-layouts  1.97 us (1%)
    all_to_all x2, waiting for transfers between devices, exchange(): lax.all_to_all(x, ('z', 'gy', 'core'), split_axis=0, concat_axis=0, tiled...  115 us
    pallas_call x1, Pallas kernels, first_sum(): pl.pallas_call(functools.partial(first_sum_kernel, group), grid_spec=pltp...  22 us
    all_to_all x2, starting transfers between devices, exchange(): lax.all_to_all(x, ('z', 'gy', 'core'), split_axis=0, concat_axis=0, tiled...  18.8 us
    pallas_call x1, Pallas kernels, terms(): pl.pallas_call(functools.partial(term_kernel, slots, capacity, places), g...  10.9 us
    pallas_call x1, Pallas kernels, first_stage(): pl.pallas_call(functools.partial(first_kernel, scale, slot, chunks, place...  7.92 us
    pallas_call x1, Pallas kernels, last_sum(): pl.pallas_call(functools.partial(last_sum_kernel, slots, places, parts),...  7.59 us
    pallas_call x1, Pallas kernels, node_stage(): pl.pallas_call(node_kernel, grid=(rows // tile,), in_specs=[node, node, p...  7.07 us
  transfers between devices with their start and end apart: 2, of which 2 were waited for; matrix products, arithmetic and copies ran while one was open for 1% of the time, Pallas kernels for 21%

profile of v5, /device:TPU:7, one launch (start us, length us, event | category | flops | bytes accessed | tf_op | source)
XLA Modules:
  0.0 193.2 jit_solution(17766271608714185947)
XLA Ops:
  0.6 7.9 %first_stage.1 = bf16[128,136,128]{2,1,0:T(8,128)(2,1)} custom-call(s32[2,384]{1,0:T(2,128)} %bitcast.11, s32[1,128]{1,0:T(1,128)} %count_ref.1, s32[64,128]{1,0:T(8,128)} %bitcast.9, bf16[128,128]{1,0:T(8,128)(2,1)} %wn_ref.1, bf16[8192,128]{1,0:T(8,128)(2,1)} %grad_ref.3, bf16[8192,128]{1,0:T(8,128)(2,1)} %pre_ref.3, bf16[8192,128]{1,0:T(8,128)(2,1)} %feat_hbm.1, ...), custom_call_target="tpu_custom_call" | custom-call | flops 1342177280 | bytes 16777216 | tf_op jit(solution)/shard_map/first_stage/pallas_call | solution.py:252
  8.6 0.0 copy-start.1
  8.6 0.0 copy-start.2
  8.6 0.0 copy-start.5
  8.6 0.0 copy-start.6
  8.6 11.2 %all-to-all-start = ((bf16[128,136,128]{2,1,0:T(8,128)(2,1)}), bf16[128,136,128]{2,1,0:T(8,128)(2,1)}, u32[]{:S(2)}, u32[]{:S(2)}) async-start(bf16[128,136,128]{2,1,0:T(8,128)(2,1)} %first_stage.1), calls=%async_computation | async-start | bytes 8912896 | tf_op jit(solution)/shard_map/all_to_all | solution.py:421
  19.8 0.1 pad.2.clone
  19.9 0.0 copy-done.1
  19.9 0.0 copy-done.2
  19.9 7.1 %node_stage.1 = (bf16[8192,128]{1,0:T(8,128)(2,1)}, bf16[64,128,128]{2,1,0:T(8,128)(2,1)S(1)}) custom-call(bf16[8192,128]{1,0:T(8,128)(2,1)} %grad_ref.3, bf16[8192,128]{1,0:T(8,128)(2,1)} %pre_ref.3, bf16[128,128]{1,0:T(8,128)(2,1)S(1)} %copy-done.2, s32[64,128]{1,0:T(8,128)S(1)} %bitcast.10), custom_call_target="tpu_custom_call" | custom-call | flops 536870912 | bytes 8388608 | tf_op jit(solution)/shard_map/node_stage/pallas_call | solution.py:69
  27.0 0.0 copy-done.5
  27.0 0.0 copy-done.6
  27.0 10.9 %terms.1 = bf16[128,264,128]{2,1,0:T(8,128)(2,1)} custom-call(s32[2,384]{1,0:T(2,128)S(1)} %bitcast.12, s32[1,128]{1,0:T(1,128)S(1)} %copy-done.6, bf16[64,128,128]{2,1,0:T(8,128)(2,1)S(1)} %get-tuple-element.9.st_ref, bf16[128,3,128,128]{3,2,1,0:T(8,128)(2,1)} %bitcast.14), custom_call_target="tpu_custom_call" | custom-call | flops 1073741824 | bytes 16777216 | tf_op jit(solution)/shard_map/terms/pallas_call | solution.py:140
  37.8 35.6 %all-to-all-done.got_ref = bf16[128,136,128]{2,1,0:T(8,128)(2,1)} async-done(((bf16[128,136,128]{2,1,0:T(8,128)(2,1)}), bf16[128,136,128]{2,1,0:T(8,128)(2,1)}, u32[]{:S(2)}, u32[]{:S(2)}) %all-to-all-start) | async-done | bytes 4456480 | tf_op jit(solution)/shard_map/all_to_all | solution.py:421
  73.5 1.1 convert_reduce_fusion
  74.6 0.1 maximum_maximum_fusion
  74.7 0.8 broadcast_dynamic-update-slice_fusion
  75.4 0.0 copy-start
  75.4 0.0 copy-start.4
  75.4 7.6 %all-to-all-start.1 = ((bf16[128,264,128]{2,1,0:T(8,128)(2,1)}), bf16[128,264,128]{2,1,0:T(8,128)(2,1)}, u32[]{:S(2)}, u32[]{:S(2)}) async-start(bf16[128,264,128]{2,1,0:T(8,128)(2,1)} %broadcast_dynamic-update-slice_fusion), calls=%async_computation.1 | async-start | bytes 17301504 | tf_op jit(solution)/shard_map/all_to_all | solution.py:421
  83.1 1.0 slice.19
  84.1 0.1 copy.17
  84.2 0.0 copy-done
  84.2 0.0 copy-done.4
  84.2 0.0 copy-start.3
  84.2 22.0 %first_sum.1.base_hbm = f32[64,128,128]{2,1,0:T(8,128)} custom-call(s32[8,128]{1,0:T(8,128)S(1)} %convert_bitcast_fusion.cols_ref, bf16[128,136,128]{2,1,0:T(8,128)(2,1)} %all-to-all-done.got_ref, bf16[8192,128]{1,0:T(8,128)(2,1)S(1)} %copy-done, bf16[8192,128]{1,0:T(8,128)(2,1)} %pre_ref.3, bf16[128,128]{1,0:T(8,128)(2,1)S(1)} %copy-done.4), custom_call_target="tpu_custom_call" | custom-call | flops 268435456 | bytes 12845056 | tf_op jit(solution)/shard_map/first_sum/pallas_call | solution.py:310
  106.2 0.0 copy-done.3
  106.2 79.4 %all-to-all-done.1.got_hbm = bf16[128,264,128]{2,1,0:T(8,128)(2,1)} async-done(((bf16[128,264,128]{2,1,0:T(8,128)(2,1)}), bf16[128,264,128]{2,1,0:T(8,128)(2,1)}, u32[]{:S(2)}, u32[]{:S(2)}) %all-to-all-start.1) | async-done | bytes 8650784 | tf_op jit(solution)/shard_map/all_to_all | solution.py:421
  185.6 7.6 %last_sum.1 = (bf16[64,128,128]{2,1,0:T(8,128)(2,1)}, f32[128,128]{1,0:T(8,128)}, f32[128,128]{1,0:T(8,128)}) custom-call(s32[8,128]{1,0:T(8,128)} %copy-done.3, bf16[128,264,128]{2,1,0:T(8,128)(2,1)} %all-to-all-done.1.got_hbm, f32[64,128,128]{2,1,0:T(8,128)} %first_sum.1.base_hbm), custom_call_target="tpu_custom_call" | custom-call | flops 4325376 | bytes 14942208 | tf_op jit(solution)/shard_map/last_sum/pallas_call | solution.py:395
  (3 shorter events, 0.0 us)
Async XLA Ops:
  8.6 11.3 %copy-start.1 = (s32[8192]{0:T(1024)S(1)}, s32[8192]{0:T(1024)}, u32[]{:S(2)}) copy-start(s32[8192]{0:T(1024)} %param.16) | copy-start | bytes 98308
  8.6 11.3 %copy-start.2 = (bf16[128,128]{1,0:T(8,128)(2,1)S(1)}, bf16[128,128]{1,0:T(8,128)(2,1)}, u32[]{:S(2)}) copy-start(bf16[128,128]{1,0:T(8,128)(2,1)} %wn_ref.1) | copy-start | bytes 98308
  8.6 18.4 %copy-start.5 = (s32[1,2,384]{2,1,0:T(2,128)S(1)}, s32[1,2,384]{2,1,0:T(2,128)}, u32[]{:S(2)}) copy-start(s32[1,2,384]{2,1,0:T(2,128)} %param.18) | copy-start | bytes 9220
  8.6 18.4 %copy-start.6 = (s32[1,128]{1,0:T(1,128)S(1)}, s32[1,128]{1,0:T(1,128)}, u32[]{:S(2)}) copy-start(s32[1,128]{1,0:T(1,128)} %count_ref.1) | copy-start | bytes 1540
  8.6 64.9 %all-to-all-start = ((bf16[128,136,128]{2,1,0:T(8,128)(2,1)}), bf16[128,136,128]{2,1,0:T(8,128)(2,1)}, u32[]{:S(2)}, u32[]{:S(2)}) async-start(bf16[128,136,128]{2,1,0:T(8,128)(2,1)} %first_stage.1), calls=%async_computation | async-start | bytes 8912896 | tf_op jit(solution)/shard_map/all_to_all | solution.py:421
  75.4 8.8 %copy-start = (bf16[8192,128]{1,0:T(8,128)(2,1)S(1)}, bf16[8192,128]{1,0:T(8,128)(2,1)}, u32[]{:S(2)}) copy-start(bf16[8192,128]{1,0:T(8,128)(2,1)} %grad_ref.3) | copy-start | bytes 6291460
  75.4 8.8 %copy-start.4 = (bf16[128,128]{1,0:T(8,128)(2,1)S(1)}, bf16[128,128]{1,0:T(8,128)(2,1)}, u32[]{:S(2)}) copy-start(bf16[128,128]{1,0:T(8,128)(2,1)} %ws_ref.1) | copy-start | bytes 98308
  75.4 110.2 %all-to-all-start.1 = ((bf16[128,264,128]{2,1,0:T(8,128)(2,1)}), bf16[128,264,128]{2,1,0:T(8,128)(2,1)}, u32[]{:S(2)}, u32[]{:S(2)}) async-start(bf16[128,264,128]{2,1,0:T(8,128)(2,1)} %broadcast_dynamic-update-slice_fusion), calls=%async_computation.1 | async-start | bytes 17301504 | tf_op jit(solution)/shard_map/all_to_all | solution.py:421
  84.2 22.0 %copy-start.3 = (s32[8,128]{1,0:T(8,128)}, s32[8,128]{1,0:T(8,128)S(1)}, u32[]{:S(2)}) copy-start(s32[8,128]{1,0:T(8,128)S(1)} %convert_bitcast_fusion.cols_ref) | copy-start | bytes 12292

commit v6 on v5

--- a/solution.py
+++ b/solution.py
@@ -329,8 +329,8 @@
 
 
 def last_sum_kernel(
-    slots, places, parts, cols_ref, got_hbm, base_hbm, out_hbm, gs_ref, gn_ref,
-    got, out, base, acc, gw, got_sem, base_sem, out_sem,
+    slots, places, parts, cols_hbm, got_hbm, base_hbm, out_hbm, gs_ref, gn_ref,
+    cols_ref, got, out, base, acc, gw, cols_sem, got_sem, base_sem, out_sem,
 ):
     peers = got.shape[0]
     blocks, block, width = acc.shape
@@ -347,6 +347,8 @@
         return pltpu.make_async_copy(out.at[at], out_hbm.at[at], out_sem.at[p])
 
     load = pltpu.make_async_copy(base_hbm, base, base_sem)
+    cols_load = pltpu.make_async_copy(cols_hbm, cols_ref, cols_sem)
+    cols_load.start()
     for g in range(groups):
         got_copy(g).start()
     load.start()
@@ -354,6 +356,8 @@
     @pl.loop(0, blocks, unroll=4)
     def _(b):
         acc[b] = jnp.zeros((block, width), F32)
+
+    cols_load.wait()
 
     @pl.loop(0, groups)
     def _(g):
@@ -394,14 +398,16 @@
     vmem = pl.BlockSpec(memory_space=pltpu.VMEM)
     return pl.pallas_call(
         functools.partial(last_sum_kernel, slots, places, parts),
-        in_specs=[pl.BlockSpec(memory_space=pltpu.SMEM), hbm, hbm],
+        in_specs=[hbm, hbm, hbm],
         out_specs=[hbm, vmem, vmem],
         scratch_shapes=[
+            pltpu.SMEM(cols.shape, jnp.int32),
             pltpu.VMEM((peers, rows, width), BF16),
             pltpu.VMEM((blocks, block, width), BF16),
             pltpu.VMEM((blocks, block, width), F32),
             pltpu.VMEM((blocks, block, width), F32),
             pltpu.VMEM((width, 2 * width), F32),
+            pltpu.SemaphoreType.DMA,
             pltpu.SemaphoreType.DMA((groups,)),
             pltpu.SemaphoreType.DMA,
             pltpu.SemaphoreType.DMA((parts,)),

time: 194 us -> 194 us (level)
  no operation moved by 1% of the time
where the time goes in v6:
time: 194 us; the launch traced here: 192 us
  waiting for transfers between devices  115 us (59%)
  Pallas kernels  54.8 us (28%)
  starting transfers between devices  18.8 us (10%)
  local copies, waits for them, and re-layouts  1.97 us (1%)
    all_to_all x2, waiting for transfers between devices, exchange(): lax.all_to_all(x, ('z', 'gy', 'core'), split_axis=0, concat_axis=0, tiled...  115 us
    pallas_call x1, Pallas kernels, first_sum(): pl.pallas_call(functools.partial(first_sum_kernel, group), grid_spec=pltp...  22 us
    all_to_all x2, starting transfers between devices, exchange(): lax.all_to_all(x, ('z', 'gy', 'core'), split_axis=0, concat_axis=0, tiled...  18.8 us
    pallas_call x1, Pallas kernels, terms(): pl.pallas_call(functools.partial(term_kernel, slots, capacity, places), g...  10.9 us
    pallas_call x1, Pallas kernels, first_stage(): pl.pallas_call(functools.partial(first_kernel, scale, slot, chunks, place...  7.92 us
    pallas_call x1, Pallas kernels, node_stage(): pl.pallas_call(node_kernel, grid=(rows // tile,), in_specs=[node, node, p...  7.07 us
    pallas_call x1, Pallas kernels, last_sum(): pl.pallas_call(functools.partial(last_sum_kernel, slots, places, parts),...  6.87 us
  transfers between devices with their start and end apart: 2, of which 2 were waited for; matrix products, arithmetic and copies ran while one was open for 1% of the time, Pallas kernels for 21%

profile of v6, /device:TPU:7, one launch (start us, length us, event | category | flops | bytes accessed | tf_op | source)
XLA Modules:
  0.0 192.5 jit_solution(4725673878491171292)
XLA Ops:
  0.6 7.9 %first_stage.1 = bf16[128,136,128]{2,1,0:T(8,128)(2,1)} custom-call(s32[2,384]{1,0:T(2,128)} %bitcast.11, s32[1,128]{1,0:T(1,128)} %count_ref.1, s32[64,128]{1,0:T(8,128)} %bitcast.9, bf16[128,128]{1,0:T(8,128)(2,1)} %wn_ref.1, bf16[8192,128]{1,0:T(8,128)(2,1)} %grad_ref.3, bf16[8192,128]{1,0:T(8,128)(2,1)} %pre_ref.3, bf16[8192,128]{1,0:T(8,128)(2,1)} %feat_hbm.1, ...), custom_call_target="tpu_custom_call" | custom-call | flops 1342177280 | bytes 16777216 | tf_op jit(solution)/shard_map/first_stage/pallas_call | solution.py:252
  8.6 0.0 copy-start.1
  8.6 0.0 copy-start.2
  8.6 0.0 copy-start.5
  8.6 0.0 copy-start.6
  8.6 11.2 %all-to-all-start = ((bf16[128,136,128]{2,1,0:T(8,128)(2,1)}), bf16[128,136,128]{2,1,0:T(8,128)(2,1)}, u32[]{:S(2)}, u32[]{:S(2)}) async-start(bf16[128,136,128]{2,1,0:T(8,128)(2,1)} %first_stage.1), calls=%async_computation | async-start | bytes 8912896 | tf_op jit(solution)/shard_map/all_to_all | solution.py:427
  19.8 0.1 pad.2.clone
  19.9 0.0 copy-done.1
  19.9 0.0 copy-done.2
  19.9 7.1 %node_stage.1 = (bf16[8192,128]{1,0:T(8,128)(2,1)}, bf16[64,128,128]{2,1,0:T(8,128)(2,1)S(1)}) custom-call(bf16[8192,128]{1,0:T(8,128)(2,1)} %grad_ref.3, bf16[8192,128]{1,0:T(8,128)(2,1)} %pre_ref.3, bf16[128,128]{1,0:T(8,128)(2,1)S(1)} %copy-done.2, s32[64,128]{1,0:T(8,128)S(1)} %bitcast.10), custom_call_target="tpu_custom_call" | custom-call | flops 536870912 | bytes 8388608 | tf_op jit(solution)/shard_map/node_stage/pallas_call | solution.py:69
  27.0 0.0 copy-done.5
  27.0 0.0 copy-done.6
  27.0 10.9 %terms.1 = bf16[128,264,128]{2,1,0:T(8,128)(2,1)} custom-call(s32[2,384]{1,0:T(2,128)S(1)} %bitcast.12, s32[1,128]{1,0:T(1,128)S(1)} %copy-done.6, bf16[64,128,128]{2,1,0:T(8,128)(2,1)S(1)} %get-tuple-element.9.st_ref, bf16[128,3,128,128]{3,2,1,0:T(8,128)(2,1)} %bitcast.14), custom_call_target="tpu_custom_call" | custom-call | flops 1073741824 | bytes 16777216 | tf_op jit(solution)/shard_map/terms/pallas_call | solution.py:140
  37.8 35.6 %all-to-all-done.got_ref = bf16[128,136,128]{2,1,0:T(8,128)(2,1)} async-done(((bf16[128,136,128]{2,1,0:T(8,128)(2,1)}), bf16[128,136,128]{2,1,0:T(8,128)(2,1)}, u32[]{:S(2)}, u32[]{:S(2)}) %all-to-all-start) | async-done | bytes 4456480 | tf_op jit(solution)/shard_map/all_to_all | solution.py:427
  73.5 1.1 convert_reduce_fusion
  74.6 0.1 maximum_maximum_fusion
  74.7 0.8 broadcast_dynamic-update-slice_fusion
  75.4 0.0 copy-start
  75.4 0.0 copy-start.4
  75.4 7.6 %all-to-all-start.1 = ((bf16[128,264,128]{2,1,0:T(8,128)(2,1)}), bf16[128,264,128]{2,1,0:T(8,128)(2,1)}, u32[]{:S(2)}, u32[]{:S(2)}) async-start(bf16[128,264,128]{2,1,0:T(8,128)(2,1)} %broadcast_dynamic-update-slice_fusion), calls=%async_computation.1 | async-start | bytes 17301504 | tf_op jit(solution)/shard_map/all_to_all | solution.py:427
  83.1 1.0 slice.19
  84.1 0.1 copy.17
  84.2 0.0 copy-done
  84.2 0.0 copy-done.4
  84.2 0.0 copy-start.3
  84.2 22.0 %first_sum.1.base_hbm = f32[64,128,128]{2,1,0:T(8,128)} custom-call(s32[8,128]{1,0:T(8,128)S(1)} %convert_bitcast_fusion.cols_ref.cols_hbm, bf16[128,136,128]{2,1,0:T(8,128)(2,1)} %all-to-all-done.got_ref, bf16[8192,128]{1,0:T(8,128)(2,1)S(1)} %copy-done, bf16[8192,128]{1,0:T(8,128)(2,1)} %pre_ref.3, bf16[128,128]{1,0:T(8,128)(2,1)S(1)} %copy-done.4), custom_call_target="tpu_custom_call" | custom-call | flops 268435456 | bytes 12845056 | tf_op jit(solution)/shard_map/first_sum/pallas_call | solution.py:310
  106.2 0.0 copy-done.3
  106.2 79.4 %all-to-all-done.1.got_hbm = bf16[128,264,128]{2,1,0:T(8,128)(2,1)} async-done(((bf16[128,264,128]{2,1,0:T(8,128)(2,1)}), bf16[128,264,128]{2,1,0:T(8,128)(2,1)}, u32[]{:S(2)}, u32[]{:S(2)}) %all-to-all-start.1) | async-done | bytes 8650784 | tf_op jit(solution)/shard_map/all_to_all | solution.py:427
  185.6 6.9 %last_sum.1 = (bf16[64,128,128]{2,1,0:T(8,128)(2,1)}, f32[128,128]{1,0:T(8,128)}, f32[128,128]{1,0:T(8,128)}) custom-call(s32[8,128]{1,0:T(8,128)} %copy-done.3, bf16[128,264,128]{2,1,0:T(8,128)(2,1)} %all-to-all-done.1.got_hbm, f32[64,128,128]{2,1,0:T(8,128)} %first_sum.1.base_hbm), custom_call_target="tpu_custom_call" | custom-call | flops 4325376 | bytes 14942208 | tf_op jit(solution)/shard_map/last_sum/pallas_call | solution.py:399
  (3 shorter events, 0.0 us)
Async XLA Ops:
  8.6 11.3 %copy-start.1 = (s32[8192]{0:T(1024)S(1)}, s32[8192]{0:T(1024)}, u32[]{:S(2)}) copy-start(s32[8192]{0:T(1024)} %param.16) | copy-start | bytes 98308
  8.6 11.3 %copy-start.2 = (bf16[128,128]{1,0:T(8,128)(2,1)S(1)}, bf16[128,128]{1,0:T(8,128)(2,1)}, u32[]{:S(2)}) copy-start(bf16[128,128]{1,0:T(8,128)(2,1)} %wn_ref.1) | copy-start | bytes 98308
  8.6 18.4 %copy-start.5 = (s32[1,2,384]{2,1,0:T(2,128)S(1)}, s32[1,2,384]{2,1,0:T(2,128)}, u32[]{:S(2)}) copy-start(s32[1,2,384]{2,1,0:T(2,128)} %param.18) | copy-start | bytes 9220
  8.6 18.4 %copy-start.6 = (s32[1,128]{1,0:T(1,128)S(1)}, s32[1,128]{1,0:T(1,128)}, u32[]{:S(2)}) copy-start(s32[1,128]{1,0:T(1,128)} %count_ref.1) | copy-start | bytes 1540
  8.6 64.9 %all-to-all-start = ((bf16[128,136,128]{2,1,0:T(8,128)(2,1)}), bf16[128,136,128]{2,1,0:T(8,128)(2,1)}, u32[]{:S(2)}, u32[]{:S(2)}) async-start(bf16[128,136,128]{2,1,0:T(8,128)(2,1)} %first_stage.1), calls=%async_computation | async-start | bytes 8912896 | tf_op jit(solution)/shard_map/all_to_all | solution.py:427
  75.4 8.8 %copy-start = (bf16[8192,128]{1,0:T(8,128)(2,1)S(1)}, bf16[8192,128]{1,0:T(8,128)(2,1)}, u32[]{:S(2)}) copy-start(bf16[8192,128]{1,0:T(8,128)(2,1)} %grad_ref.3) | copy-start | bytes 6291460
  75.4 8.8 %copy-start.4 = (bf16[128,128]{1,0:T(8,128)(2,1)S(1)}, bf16[128,128]{1,0:T(8,128)(2,1)}, u32[]{:S(2)}) copy-start(bf16[128,128]{1,0:T(8,128)(2,1)} %ws_ref.1) | copy-start | bytes 98308
  75.4 110.2 %all-to-all-start.1 = ((bf16[128,264,128]{2,1,0:T(8,128)(2,1)}), bf16[128,264,128]{2,1,0:T(8,128)(2,1)}, u32[]{:S(2)}, u32[]{:S(2)}) async-start(bf16[128,264,128]{2,1,0:T(8,128)(2,1)} %broadcast_dynamic-update-slice_fusion), calls=%async_computation.1 | async-start | bytes 17301504 | tf_op jit(solution)/shard_map/all_to_all | solution.py:427
  84.2 22.0 %copy-start.3 = (s32[8,128]{1,0:T(8,128)}, s32[8,128]{1,0:T(8,128)S(1)}, u32[]{:S(2)}) copy-start(s32[8,128]{1,0:T(8,128)S(1)} %convert_bitcast_fusion.cols_ref.cols_hbm) | copy-start | bytes 12292
